TPU v7x, 512 devices: a whole 4x8x8 slice. The times are simulated.
512 devices in a mesh: dp: 32 (over z, x), tensor: 16 (over y, core).
Axes of the slice: x: 4, y: 8, z: 8, core: 2. Of those that a mesh axis runs over, the one named last changes fastest.
Arguments:
- tokens: bfloat16 [512, 8192], P('dp', 'tensor'), may hold values from -6 to 6
- cotangent: bfloat16 [512, 8192], P('dp', 'tensor'), may hold values from -6 to 6
- token_class: int32 [512], P('dp'), may hold values from 0 to 3
- class_bands: int32 [4], replicated, may hold values from 1 to 32, as said below
- mantissas: bfloat16 [3, 28672, 8192], P(None, 'dp', 'tensor'), may hold values from -0.0625 to 0.0625
- exponents: int32 [3, 224, 64], P(None, 'dp', 'tensor'), may hold values from -2 to 1
Outputs:
- mixed: bfloat16 [512, 8192], P('dp', 'tensor')
- input_grad: bfloat16 [512, 8192], P('dp', 'tensor')
- down_grad: bfloat16 [28672, 8192], P('dp', 'tensor')
Inputs may be any that keep to these rules, and one draw needn't show every extreme that they name: `class_bands`: some class uses all 32 bands.
All inputs are finite; a program needn't handle non-finite values.
Results may differ from a plain program's by a relative error of at most 0.0085.
Values may be sent and summed in bfloat16 or wider, within the bound.
No kernel may reach another device: no remote copies, remote signals or barrier semaphores. Data moves between devices by JAX's collectives and lax.ppermute only.
A program may use at most 64 MiB of HBM per device.

v0:
```python
import jax
import jax.numpy as jnp
from jax import lax
from jax.sharding import PartitionSpec as P


def dequant_local(mantissas, exponents):
    mats, rows, cols = mantissas.shape
    block = rows // exponents.shape[1]
    scale = jnp.exp2(exponents.astype(jnp.float32)).astype(mantissas.dtype)
    blocks = (
        mantissas.reshape(mats, rows // block, block, cols // block, block)
        * scale[:, :, None, :, None]
    )
    return blocks.reshape(mats, rows, cols)


def activate(gate, up, dh, width, first):
    units = first + jnp.arange(gate.shape[1], dtype=jnp.int32)
    keep = (units[None, :] < width[:, None]).astype(jnp.float32)
    sig = jax.nn.sigmoid(gate)
    silu = gate * sig
    hidden = (keep * silu * up).astype(jnp.bfloat16)
    dgate = (keep * dh * up * sig * (1.0 + gate * (1.0 - sig))).astype(jnp.bfloat16)
    dup = (keep * dh * silu).astype(jnp.bfloat16)
    return (hidden, dgate, dup)


def body(tokens, cotangent, token_class, class_bands, mantissas, exponents):
    band_rows = mantissas.shape[1]
    x_all, dy_all, classes = (
        lax.all_gather(tokens, "dp", axis=0, tiled=True),
        lax.all_gather(cotangent, "dp", axis=0, tiled=True),
        lax.all_gather(token_class, "dp", axis=0, tiled=True),
    )
    weights = dequant_local(mantissas, exponents)
    gate_w = weights[0]
    up_w = weights[1]
    down_w = weights[2]
    lookup = (
        classes[:, None] == jnp.arange(class_bands.shape[0], dtype=jnp.int32)[None, :]
    ).astype(jnp.int32)
    width = jnp.sum(lookup * class_bands[None, :], axis=1) * band_rows
    first = lax.axis_index("dp") * band_rows
    contract = (((1,), (1,)), ((), ()))
    gate_part = lax.dot_general(x_all, gate_w, contract, preferred_element_type=jnp.float32)
    up_part = lax.dot_general(x_all, up_w, contract, preferred_element_type=jnp.float32)
    dh_part = lax.dot_general(dy_all, down_w, contract, preferred_element_type=jnp.float32)
    gate, up, dh = lax.psum((gate_part, up_part, dh_part), "tensor")
    hidden, dgate, dup = activate(gate, up, dh, width, first)
    out_part = jnp.dot(hidden, down_w, preferred_element_type=jnp.float32)
    grad_part = jnp.dot(dgate, gate_w, preferred_element_type=jnp.float32) + jnp.dot(
        dup, up_w, preferred_element_type=jnp.float32
    )
    mixed, input_grad = (
        lax.psum_scatter(out_part, "dp", scatter_dimension=0, tiled=True),
        lax.psum_scatter(grad_part, "dp", scatter_dimension=0, tiled=True),
    )
    norm_factor = 1.0 / jnp.sqrt(jnp.float32(x_all.shape[0]))
    down_grad = (
        lax.dot_general(
            hidden, dy_all, (((0,), (0,)), ((), ())), preferred_element_type=jnp.float32
        )
        * norm_factor
    )
    return (
        mixed.astype(jnp.bfloat16),
        input_grad.astype(jnp.bfloat16),
        down_grad.astype(jnp.bfloat16),
    )


def solution(mesh):
    in_specs = (
        P("dp", "tensor"),
        P("dp", "tensor"),
        P("dp"),
        P(),
        P(None, "dp", "tensor"),
        P(None, "dp", "tensor"),
    )
    out_specs = (P("dp", "tensor"), P("dp", "tensor"), P("dp", "tensor"))
    return jax.shard_map(body, mesh=mesh, in_specs=in_specs, out_specs=out_specs, check_vma=False)
```

profile of v0, /device:TPU:1, one launch (start us, length us, event | category | flops | bytes accessed | tf_op | source)
XLA Modules:
  0.0 706.2 jit_solution(5415804434028158964)
XLA Ops:
  7.2 0.0 copy-start.3
  7.2 0.0 all-reduce.4.cloned.1.call-start
  7.2 4.6 reshape.26
  11.9 0.0 copy-done.3
  11.9 0.1 copy.10
  12.0 1.2 broadcast_multiply_fusion
  13.3 0.0 copy-start.1
  13.3 0.0 copy-start.2
  13.3 1.2 fusion.25
  14.5 0.0 copy-done.1
  14.5 44.3 %all_gather.11 = bf16[512,512]{1,0:T(8,128)(2,1)S(1)} all-gather(bf16[16,512]{1,0:T(8,128)(2,1)S(1)} %copy-done.1), channel_id=1, replica_groups=mesh['dp'=32,'tensor'=16] {'dp'}, dimensions={0}, use_global_device_ids=true | all-gather | bytes 540672 | tf_op jit(solution)/shard_map/all_gather | solution.py:33
  58.8 0.0 copy-done.2
  58.8 36.8 %all_gather.10 = bf16[512,512]{1,0:T(8,128)(2,1)S(1)} all-gather(bf16[16,512]{1,0:T(8,128)(2,1)S(1)} %copy-done.2), channel_id=1, replica_groups=mesh['dp'=32,'tensor'=16] {'dp'}, dimensions={0}, use_global_device_ids=true | all-gather | bytes 540672 | tf_op jit(solution)/shard_map/all_gather | solution.py:32
  95.6 1.9 convolution_bitcast_fusion.1
  97.6 2.0 convolution_bitcast_fusion.2
  99.6 1.9 convolution_bitcast_fusion
  101.5 0.0 copy-start.6
  101.5 0.0 copy-start.4
  101.5 0.0 all-reduce.4.cloned.1.call-update
  101.5 0.0 reduce-scatter.5.cloned.1.call-start
  101.6 1.3 dynamic-slice
  103.5 0.0 copy-done.6
  103.5 0.2 dynamic-update-slice
  103.8 13.7 %all-reduce = s32[512]{0:T(512)S(1)} all-reduce(s32[512]{0:T(512)S(1)} %dynamic-update-slice), channel_id=1, replica_groups=mesh['dp'=32,'tensor'=16] {'dp'}, use_global_device_ids=true, to_apply=%add | all-reduce | flops 512 | bytes 4096
  117.4 0.0 copy-done.4
  117.4 0.1 select_reduce_fusion
  117.5 134.6 %all-reduce.4.cloned.1.call-done = (f32[512,896]{0,1:T(8,128)}, f32[512,896]{0,1:T(8,128)}, f32[512,896]{0,1:T(8,128)}) async-done(((f32[512,896]{0,1:T(8,128)}, f32[512,896]{0,1:T(8,128)}, f32[512,896]{0,1:T(8,128)}), (f32[512,896]{0,1:T(8,128)}, f32[512,896]{0,1:T(8,128)}, f32[512,896]{0,1:T(8,128)})) %all-reduce.4.cloned.1.call-update) | async-done | bytes 5505040 | tf_op jit(solution)/shard_map/psum | solution.py:49
  252.1 0.0 copy-start
  252.1 0.0 copy-start.5
  252.1 4.1 fusion.8
  256.2 0.0 copy-done
  256.2 0.0 copy-done.5
  256.2 2.1 convolution_add_fusion
  258.3 0.0 reduce-scatter.5.cloned.1.call-update
  258.4 0.0 reduce-scatter.3.cloned.1.call-start
  258.4 2.6 fusion.1
  261.0 1.7 fusion.4
  262.7 0.0 reduce-scatter.3.cloned.1.call-update
  262.7 1.6 multiply_convert_fusion
  264.3 210.7 %reduce-scatter.5.cloned.1.call-done = f32[16,512]{1,0:T(8,128)} async-done(((f32[512,512]{1,0:T(8,128)}), f32[16,512]{1,0:T(8,128)}) %reduce-scatter.5.cloned.1.call-update) | async-done | bytes 32784 | tf_op jit(solution)/shard_map/reduce_scatter | solution.py:57
  475.0 1.4 convert_element_type.32
  476.4 221.9 %reduce-scatter.3.cloned.1.call-done = f32[16,512]{1,0:T(8,128)} async-done(((f32[512,512]{1,0:T(8,128)}), f32[16,512]{1,0:T(8,128)}) %reduce-scatter.3.cloned.1.call-update) | async-done | bytes 32784 | tf_op jit(solution)/shard_map/reduce_scatter | solution.py:56
  698.3 1.4 convert_element_type.29
  (4 shorter events, 0.0 us)
Async XLA Ops:
  7.2 4.7 copy-start.3
  7.2 244.9 %all-reduce.4.cloned.1.call-start = ((), (), s32[]{:S(2)}) async-start(), calls=%async_computation.4 | async-start | bytes 11010048 | tf_op jit(solution)/shard_map/psum | solution.py:49
  13.3 1.2 copy-start.1
  13.3 45.5 %copy-start.2 = (bf16[16,512]{1,0:T(8,128)(2,1)S(1)}, bf16[16,512]{1,0:T(8,128)(2,1)}, u32[]{:S(2)}) copy-start(bf16[16,512]{1,0:T(8,128)(2,1)} %param.6) | copy-start | bytes 49156
  101.5 2.0 copy-start.6
  101.5 15.9 %copy-start.4 = (s32[4]{0:T(128)S(1)}, s32[4]{0:T(128)}, u32[]{:S(2)}) copy-start(s32[4]{0:T(128)} %param.9) | copy-start | bytes 52
  101.5 373.5 %reduce-scatter.5.cloned.1.call-start = ((), (), s32[]{:S(2)}) async-start(), calls=%async_computation.3 | async-start | bytes 1081344 | tf_op jit(solution)/shard_map/reduce_scatter | solution.py:57
  252.1 4.1 copy-start
  252.1 4.1 copy-start.5
  258.4 439.9 %reduce-scatter.3.cloned.1.call-start = ((), (), s32[]{:S(2)}) async-start(), calls=%async_computation.2 | async-start | bytes 1081344 | tf_op jit(solution)/shard_map/reduce_scatter | solution.py:56
Sparse Core Ops, SparseCore 0:
  101.6 150.4 all-reduce.3
  258.5 216.4 reduce-scatter.4
  480.0 218.1 reduce-scatter.2
where the time goes:
time: 711 us; the launch traced here: 706 us
  waiting for transfers between devices  567 us (80%)
  blocking collectives  94.8 us (13%)
  matrix products  15.3 us (2%)
  between operations  14.5 us (2%)
  local copies, waits for them, and re-layouts  7.48 us (1%)
    reduce_scatter x1, waiting for transfers between devices, body(): lax.psum_scatter(out_part, 'dp', scatter_dimension=0, tiled=True)  222 us
    reduce_scatter x1, waiting for transfers between devices, body(): lax.psum_scatter(grad_part, 'dp', scatter_dimension=0, tiled=True)  211 us
    psum x1, waiting for transfers between devices, body(): gate, up, dh = lax.psum((gate_part, up_part, dh_part), 'tensor')  135 us
    all_gather x1, blocking collectives, body(): lax.all_gather(cotangent, 'dp', axis=0, tiled=True)  44.3 us
    all_gather x1, blocking collectives, body(): lax.all_gather(tokens, 'dp', axis=0, tiled=True)  36.8 us
  transfers between devices with their start and end apart: 3, of which 3 were waited for; matrix products, arithmetic and copies ran while one was open for 1% of the time, Pallas kernels for 0%

commit v1 on v0

v1 whole, which is shorter than its diff:
```python
import jax
import jax.numpy as jnp
from jax import lax
from jax.experimental import pallas as pl
from jax.experimental.pallas import tpu as pltpu
from jax.sharding import Mesh
from jax.sharding import PartitionSpec as P

BLOCK = 128
SWAP = [(0, 1), (1, 0)]
NT = (((1,), (1,)), ((), ()))
TN = (((0,), (0,)), ((), ()))
F32 = jnp.float32
BF16 = jnp.bfloat16


def call(kernel, name, outs, args, smem=(), flops=0, moved=0):
    vmem = pl.BlockSpec(memory_space=pltpu.VMEM)
    scalar = pl.BlockSpec(memory_space=pltpu.SMEM)
    return pl.pallas_call(
        kernel,
        name=name,
        out_shape=outs,
        in_specs=[scalar if i in smem else vmem for i in range(len(args))],
        out_specs=vmem,
        cost_estimate=pl.CostEstimate(flops=flops, bytes_accessed=moved, transcendentals=0),
        compiler_params=pltpu.CompilerParams(vmem_limit_bytes=32 * 1024 * 1024),
    )(*args)


def dequant_kernel(scale, mant, out):
    mats, rows, cols = mant.shape
    for m in range(mats):
        for r in range(rows // BLOCK):
            for c in range(cols // BLOCK):
                at = (m, pl.ds(r * BLOCK, BLOCK), pl.ds(c * BLOCK, BLOCK))
                out[at] = (mant[at].astype(F32) * scale[m, r, c]).astype(BF16)


def project_kernel(tokens, own, other, out):
    senders, rows, width = tokens.shape
    half = width // 2
    units = own.shape[1]
    wide = tokens[...].astype(F32).reshape(senders, 2, rows // 2, width)
    x = wide[:, 0].reshape(-1, width).astype(BF16)
    dy = wide[:, 1].reshape(-1, width).astype(BF16)
    for m, left in ((0, x), (1, x), (2, dy)):
        term = lax.dot_general(left[:, :half], own[m], NT, preferred_element_type=F32)
        term += lax.dot_general(left[:, half:], other[m], NT, preferred_element_type=F32)
        out[:, :, m * units : (m + 1) * units] = term.astype(BF16).reshape(out.shape[0], out.shape[1], units)


def activate_kernel(parts, out):
    copies, _, three = parts.shape
    units = three // 3
    total = jnp.sum(parts[...].astype(F32), axis=0)
    gate, up, dh = total[:, :units], total[:, units : 2 * units], total[:, 2 * units :]
    sig = jax.nn.sigmoid(gate)
    silu = gate * sig
    hidden = (silu * up).astype(BF16)
    dgate = (dh * up * sig * (1.0 + gate * (1.0 - sig))).astype(BF16)
    dup = (dh * silu).astype(BF16)
    for i in range(copies):
        out[i, :, :units] = hidden
        out[i, :, units : 2 * units] = dgate
        out[i, :, 2 * units :] = dup


def expand_kernel(acts, own, other, out):
    units = own.shape[1]
    owners, rows, width = out.shape
    half = width // 2
    hidden = acts[:, :, :units].reshape(-1, units)
    dgate = acts[:, :, units : 2 * units].reshape(-1, units)
    dup = acts[:, :, 2 * units :].reshape(-1, units)
    for start, w in ((0, own), (half, other)):
        mixed = jnp.dot(hidden, w[2], preferred_element_type=F32)
        grad = jnp.dot(dgate, w[0], preferred_element_type=F32)
        grad += jnp.dot(dup, w[1], preferred_element_type=F32)
        both = jnp.concatenate(
            [mixed.reshape(owners, rows // 2, half), grad.reshape(owners, rows // 2, half)], axis=1
        )
        out[:, :, start : start + half] = both.astype(BF16)


def body(tokens, cotangent, token_class, class_bands, mantissas, exponents):
    bands = lax.axis_size("dp")
    lines = lax.axis_size("y")
    core = lax.axis_index("c")
    rows, half = tokens.shape
    mine = rows // 2
    units = mantissas.shape[1]

    pair = jnp.stack([tokens.reshape(2, mine, half), cotangent.reshape(2, mine, half)], axis=1)
    keep_part = lax.dynamic_index_in_dim(pair, core, 0, False).reshape(rows, half)
    send_part = lax.dynamic_index_in_dim(pair, 1 - core, 0, False).reshape(rows, half)
    got_part = lax.ppermute(send_part, "c", SWAP)
    block = jnp.concatenate([keep_part, got_part], axis=1)
    classes = lax.dynamic_slice_in_dim(token_class, core * mine, mine)
    lookup = classes[:, None] == jnp.arange(class_bands.shape[0], dtype=jnp.int32)[None, :]
    used = jnp.sum(jnp.where(lookup, class_bands[None, :], 0), axis=1)
    used = jnp.concatenate([used, used])
    band = jnp.arange(bands, dtype=jnp.int32)
    masked = jnp.where((band[:, None] < used[None, :])[:, :, None], block[None], 0)
    gathered = lax.all_to_all(masked, "dp", 0, 0, tiled=True)

    scale = jnp.exp2(exponents.astype(F32)).astype(BF16).astype(F32)
    own = call(dequant_kernel, "dequant", jax.ShapeDtypeStruct(mantissas.shape, BF16), (scale, mantissas),
               smem=(0,), flops=mantissas.size, moved=4 * mantissas.size)
    other = lax.ppermute(own, "c", SWAP)

    count = bands * mine
    work = 2 * count * 3 * units * 2 * half
    parts = call(project_kernel, "project", jax.ShapeDtypeStruct((lines, count // lines, 3 * units), BF16),
                 (gathered, own, other), flops=work, moved=10 << 20)
    parts = lax.all_to_all(parts, "y", 0, 0, tiled=True)
    acts = call(activate_kernel, "activate", jax.ShapeDtypeStruct(parts.shape, BF16), (parts,),
                flops=parts.size, moved=4 * parts.size)
    acts = lax.all_to_all(acts, "y", 0, 0, tiled=True)
    terms = call(expand_kernel, "expand", jax.ShapeDtypeStruct((bands, rows, 2 * half), BF16),
                 (acts, own, other), flops=work, moved=10 << 20)
    terms = lax.all_to_all(terms, "dp", 0, 0, tiled=True)

    hidden = acts[:, :, :units].reshape(count, units)
    dy = gathered[:, mine:, :].reshape(count, 2 * half)
    norm_factor = 1.0 / jnp.sqrt(jnp.float32(2 * count))
    down = lax.dot_general(hidden, dy[:, :half], TN, preferred_element_type=F32)
    away = lax.dot_general(hidden, dy[:, half:], TN, preferred_element_type=F32).astype(BF16)
    away = lax.ppermute(away, "c", SWAP)
    down_grad = ((down + away.astype(F32)) * norm_factor).astype(BF16)

    total = jnp.sum(terms.astype(F32), axis=0).astype(BF16)
    kept = total[:, :half].reshape(2, mine, half)
    got = lax.ppermute(total[:, half:], "c", SWAP).reshape(2, mine, half)
    first = jnp.where(core == 0, kept, got)
    last = jnp.where(core == 0, got, kept)
    both = jnp.concatenate([first, last], axis=1)
    return both[0], both[1], down_grad


def solution(mesh):
    dp, tensor = mesh.devices.shape
    split = Mesh(mesh.devices.reshape(dp, tensor // 2, 2), ("dp", "y", "c"))
    cols = ("y", "c")
    in_specs = (
        P("dp", cols),
        P("dp", cols),
        P("dp"),
        P(),
        P(None, "dp", cols),
        P(None, "dp", cols),
    )
    out_specs = (P("dp", cols), P("dp", cols), P("dp", cols))
    return jax.shard_map(body, mesh=split, in_specs=in_specs, out_specs=out_specs, check_vma=False)
```

time: 711 us -> 178 us (0.25)
  waiting for transfers between devices: 567 us -> 15.2 us
  starting transfers between devices: 0.12 us -> 34.6 us
  between operations: 14.5 us -> 0.8 us
  matrix products: 15.3 us -> 2.96 us
  blocking collectives: 94.8 us -> 106 us
  Pallas kernels: 0 us -> 9.07 us
    reduce_scatter x2 -> x0, waiting for transfers between devices: 433 us -> none  [the longest x1 222 us: body(): lax.psum_scatter(out_part, 'dp', scatter_dimension=0, tiled=True)]
    psum x1 -> x0, waiting for transfers between devices: 135 us -> none  [body(): gate, up, dh = lax.psum((gate_part, up_part, dh_part), 'tensor')]
    all_to_all x0 -> x3, blocking collectives: none -> 106 us  [the longest x1 38.5 us: body(): parts = lax.all_to_all(parts, 'y', 0, 0, tiled=True)]
    all_gather x2 -> x0, blocking collectives: 81.1 us -> none  [the longest x1 44.3 us: body(): lax.all_gather(cotangent, 'dp', axis=0, tiled=True)]
    ppermute x0 -> x4, starting transfers between devices: none -> 24.9 us  [the longest x1 8.77 us: body(): got_part = lax.ppermute(send_part, 'c', SWAP)]
    all_to_all x0 -> x1, waiting for transfers between devices: none -> 15.2 us  [body(): terms = lax.all_to_all(terms, 'dp', 0, 0, tiled=True)]
    unnamed x1 -> x0, blocking collectives: 13.7 us -> none
    dot_general x7 -> x2, matrix products: 15.3 us -> 2.96 us  [the longest x1 2.53 us: body(): down = lax.dot_general(hidden, dy[:, :half], TN, preferred_element_type=F32)]
  transfers between devices with their start and end apart: 3 -> 5, of which waited for: 3 -> 1; matrix products, arithmetic and copies ran while one was open for 1% -> 3% of each run, Pallas kernels for 0% -> 1%
where the time goes in v1:
time: 178 us; the launch traced here: 177 us
  blocking collectives  106 us (60%)
  starting transfers between devices  34.6 us (19%)
  waiting for transfers between devices  15.2 us (9%)
  Pallas kernels  9.07 us (5%)
  local copies, waits for them, and re-layouts  5.82 us (3%)
  matrix products  2.96 us (2%)
  other arithmetic  1.87 us (1%)
    all_to_all x1, blocking collectives, body(): parts = lax.all_to_all(parts, 'y', 0, 0, tiled=True)  38.5 us
    all_to_all x1, blocking collectives, body(): acts = lax.all_to_all(acts, 'y', 0, 0, tiled=True)  34.5 us
    all_to_all x1, blocking collectives, body(): gathered = lax.all_to_all(masked, 'dp', 0, 0, tiled=True)  33.6 us
    all_to_all x1, waiting for transfers between devices, body(): terms = lax.all_to_all(terms, 'dp', 0, 0, tiled=True)  15.2 us
    all_to_all x1, starting transfers between devices, body(): terms = lax.all_to_all(terms, 'dp', 0, 0, tiled=True)  9.68 us
    pallas_call x4, Pallas kernels, call(): pl.pallas_call(kernel, name=name, out_shape=outs, in_specs=[scalar if i i...  9.07 us
    ppermute x1, starting transfers between devices, body(): got_part = lax.ppermute(send_part, 'c', SWAP)  8.77 us
    ppermute x1, starting transfers between devices, body(): got = lax.ppermute(total[:, half:], 'c', SWAP).reshape(2, mine, half)  8.07 us
  transfers between devices with their start and end apart: 5, of which 1 were waited for; matrix products, arithmetic and copies ran while one was open for 3% of the time, Pallas kernels for 1%

profile of v1, /device:TPU:1, one launch (start us, length us, event | category | flops | bytes accessed | tf_op | source)
XLA Modules:
  0.0 176.8 jit_solution(14077711463026630453)
XLA Ops:
  0.6 0.8 fusion.10
  1.4 8.8 %collective-permute-start = (bf16[16,512]{1,0:T(8,128)(2,1)S(1)}, bf16[16,512]{1,0:T(8,128)(2,1)S(1)}, u32[]{:S(2)}, u32[]{:S(2)}) collective-permute-start(bf16[16,512]{1,0:T(8,128)(2,1)S(1)} %get-tuple-element.8), channel_id=1, source_target_pairs={{0,1},{1,0},{2,3},{3,2},{4,5},{5,4},{6,7},{7,6},{8,9},{9,8},{10,11... | collective-permute-start | bytes 49160 | tf_op jit(solution)/shard_map/ppermute | solution.py:97
  10.2 0.8 copy.10
  11.0 0.0 copy-start.4
  11.0 1.8 %copy-done.4 = bf16[3,896,512]{2,1,0:T(8,128)(2,1)S(1)} copy-done((bf16[3,896,512]{2,1,0:T(8,128)(2,1)S(1)}, bf16[3,896,512]{2,1,0:T(8,128)(2,1)}, u32[]{:S(2)}) %copy-start.4) | copy-done | bytes 2752536
  12.8 0.0 copy-start.5
  12.8 0.0 copy-start.6
  12.8 1.3 dequant.1.own
  14.0 1.9 %collective-permute-start.1 = (bf16[3,896,512]{2,1,0:T(8,128)(2,1)S(1)}, bf16[3,896,512]{2,1,0:T(8,128)(2,1)}, u32[]{:S(2)}, u32[]{:S(2)}) collective-permute-start(bf16[3,896,512]{2,1,0:T(8,128)(2,1)S(1)} %dequant.1.own), channel_id=1, source_target_pairs={{0,1},{1,0},{2,3},{3,2},{4,5},{5,4},{6,7},{7,6},{8,9},{9,8},{10,11... | collective-permute-start | bytes 8257544 | tf_op jit(solution)/shard_map/ppermute | solution.py:110
  16.0 0.0 copy-done.5
  16.0 0.1 dynamic_slice.10
  16.1 0.0 copy-done.6
  16.1 0.1 select_reduce_fusion
  16.2 0.1 pad_add_fusion
  16.2 0.0 collective-permute-done
  16.3 0.1 broadcast_select_fusion
  16.4 33.6 %all_to_all.20.tokens = bf16[32,16,1024]{2,1,0:T(8,128)(2,1)S(1)} all-to-all(bf16[32,16,1024]{2,1,0:T(8,128)(2,1)S(1)} %broadcast_select_fusion), channel_id=1, replica_groups=mesh['dp'=32,'y'=8,'c'=2] {'dp'}, dimensions={0} | all-to-all | bytes 2097152 | tf_op jit(solution)/shard_map/all_to_all | solution.py:105
  50.0 0.0 copy-start.1
  50.0 0.0 collective-permute-done.1.other
  50.0 4.0 %project.1 = bf16[8,32,2688]{2,1,0:T(8,128)(2,1)S(1)} custom-call(bf16[32,16,1024]{2,1,0:T(8,128)(2,1)S(1)} %all_to_all.20.tokens, bf16[3,896,512]{2,1,0:T(8,128)(2,1)S(1)} %dequant.1.own, bf16[3,896,512]{2,1,0:T(8,128)(2,1)} %collective-permute-done.1.other), custom_call_target="tpu_custom_call" | custom-call | flops 1409286144 | bytes 10485760 | tf_op jit(solution)/shard_map/project/pallas_call | solution.py:20
  53.9 0.0 copy-done.1
  54.0 38.5 %all_to_all.21.parts = bf16[8,32,2688]{2,1,0:T(8,128)(2,1)S(1)} all-to-all(bf16[8,32,2688]{2,1,0:T(8,128)(2,1)S(1)} %project.1), channel_id=1, replica_groups=mesh['dp'=32,'y'=8,'c'=2] {'y'}, dimensions={0} | all-to-all | bytes 2752512 | tf_op jit(solution)/shard_map/all_to_all | solution.py:116
  92.4 0.3 activate.1
  92.7 34.5 %all_to_all.22.acts = bf16[8,32,2688]{2,1,0:T(8,128)(2,1)S(1)} all-to-all(bf16[8,32,2688]{2,1,0:T(8,128)(2,1)S(1)} %activate.1), channel_id=1, replica_groups=mesh['dp'=32,'y'=8,'c'=2] {'y'}, dimensions={0} | all-to-all | bytes 2752512 | tf_op jit(solution)/shard_map/all_to_all | solution.py:119
  127.2 3.6 %expand.1 = bf16[32,16,1024]{2,1,0:T(8,128)(2,1)S(1)} custom-call(bf16[8,32,2688]{2,1,0:T(8,128)(2,1)S(1)} %all_to_all.22.acts, bf16[3,896,512]{2,1,0:T(8,128)(2,1)S(1)} %dequant.1.own, bf16[3,896,512]{2,1,0:T(8,128)(2,1)} %collective-permute-done.1.other), custom_call_target="tpu_custom_call" | custom-call | flops 1409286144 | bytes 10485760 | tf_op jit(solution)/shard_map/expand/pallas_call | solution.py:20
  130.7 0.0 copy-start
  130.7 1.1 copy-done
  131.8 0.0 copy-start.3
  131.8 1.0 copy-done.3
  132.8 0.0 copy-start.2
  132.8 9.7 %all-to-all-start.3 = ((bf16[32,16,1024]{2,1,0:T(8,128)(2,1)}), bf16[32,16,1024]{2,1,0:T(8,128)(2,1)S(1)}, u32[]{:S(2)}, u32[]{:S(2)}) async-start(bf16[32,16,1024]{2,1,0:T(8,128)(2,1)} %copy-done.3), calls=%async_computation.3 | async-start | bytes 2097152 | tf_op jit(solution)/shard_map/all_to_all | solution.py:122
  142.5 0.0 copy-done.2
  142.5 1.1 slice.36
  143.6 0.4 convolution_convert_fusion
  144.0 6.2 %collective-permute-start.3 = (bf16[896,512]{1,0:T(8,128)(2,1)S(1)}, bf16[896,512]{1,0:T(8,128)(2,1)}, u32[]{:S(2)}, u32[]{:S(2)}) collective-permute-start(bf16[896,512]{1,0:T(8,128)(2,1)S(1)} %convolution_convert_fusion), channel_id=1, source_target_pairs={{0,1},{1,0},{2,3},{3,2},{4,5},{5,4},{6,7},{7,6},{8,9},{9,8},{10,11... | collective-permute-start | bytes 2752520 | tf_op jit(solution)/shard_map/ppermute | solution.py:129
  150.2 15.2 %all-to-all-done.3 = bf16[32,16,1024]{2,1,0:T(8,128)(2,1)S(1)} async-done(((bf16[32,16,1024]{2,1,0:T(8,128)(2,1)}), bf16[32,16,1024]{2,1,0:T(8,128)(2,1)S(1)}, u32[]{:S(2)}, u32[]{:S(2)}) %all-to-all-start.3) | async-done | bytes 1048608 | tf_op jit(solution)/shard_map/all_to_all | solution.py:122
  165.4 0.2 reduce_sum.22
  165.6 8.1 %collective-permute-start.2 = (bf16[16,512]{1,0:T(8,128)(2,1)S(1)}, bf16[16,512]{1,0:T(8,128)(2,1)S(1)}, u32[]{:S(2)}, u32[]{:S(2)}) collective-permute-start(bf16[16,512]{1,0:T(8,128)(2,1)S(1)} %slice.33), channel_id=1, source_target_pairs={{0,1},{1,0},{2,3},{3,2},{4,5},{5,4},{6,7},{7,6},{8,9},{9,8},{10,11... | collective-permute-start | bytes 49160 | tf_op jit(solution)/shard_map/ppermute | solution.py:134
  173.7 0.0 collective-permute-done.3
  173.7 2.5 %multiply_convert_fusion = bf16[896,512]{1,0:T(8,128)(2,1)} fusion(bf16[896,512]{1,0:T(8,128)(2,1)} %collective-permute-done.3, bf16[256,896]{1,0:T(8,128)(2,1)S(1)} %bitcast.20, bf16[256,1024]{1,0:T(8,128)(2,1)S(1)} %slice_bitcast_fusion), kind=kOutput, calls=%fused_computation | convolution fusion | flops 236716032 | bytes 2555904 | tf_op jit(solution)/shard_map/dot_general | solution.py:127
  176.2 0.0 collective-permute-done.2
  176.2 0.6 fusion.11
  (6 shorter events, 0.1 us)
Async XLA Ops:
  1.4 14.9 %collective-permute-start = (bf16[16,512]{1,0:T(8,128)(2,1)S(1)}, bf16[16,512]{1,0:T(8,128)(2,1)S(1)}, u32[]{:S(2)}, u32[]{:S(2)}) collective-permute-start(bf16[16,512]{1,0:T(8,128)(2,1)S(1)} %get-tuple-element.8), channel_id=1, source_target_pairs={{0,1},{1,0},{2,3},{3,2},{4,5},{5,4},{6,7},{7,6},{8,9},{9,8},{10,11... | collective-permute-start | bytes 49160 | tf_op jit(solution)/shard_map/ppermute | solution.py:97
  11.0 1.8 %copy-start.4 = (bf16[3,896,512]{2,1,0:T(8,128)(2,1)S(1)}, bf16[3,896,512]{2,1,0:T(8,128)(2,1)}, u32[]{:S(2)}) copy-start(bf16[3,896,512]{2,1,0:T(8,128)(2,1)} %mant.1) | copy-start | bytes 8257540
  12.8 3.2 %copy-start.5 = (s32[16]{0:T(128)S(1)}, s32[16]{0:T(128)}, u32[]{:S(2)}) copy-start(s32[16]{0:T(128)} %param.8) | copy-start | bytes 196
  12.8 3.3 %copy-start.6 = (s32[4]{0:T(128)S(1)}, s32[4]{0:T(128)}, u32[]{:S(2)}) copy-start(s32[4]{0:T(128)} %param.9) | copy-start | bytes 52
  14.0 35.9 %collective-permute-start.1 = (bf16[3,896,512]{2,1,0:T(8,128)(2,1)S(1)}, bf16[3,896,512]{2,1,0:T(8,128)(2,1)}, u32[]{:S(2)}, u32[]{:S(2)}) collective-permute-start(bf16[3,896,512]{2,1,0:T(8,128)(2,1)S(1)} %dequant.1.own), channel_id=1, source_target_pairs={{0,1},{1,0},{2,3},{3,2},{4,5},{5,4},{6,7},{7,6},{8,9},{9,8},{10,11... | collective-permute-start | bytes 8257544 | tf_op jit(solution)/shard_map/ppermute | solution.py:110
  50.0 4.0 %copy-start.1 = (bf16[32,16,1024]{2,1,0:T(8,128)(2,1)}, bf16[32,16,1024]{2,1,0:T(8,128)(2,1)S(1)}, u32[]{:S(2)}) copy-start(bf16[32,16,1024]{2,1,0:T(8,128)(2,1)S(1)} %all_to_all.20.tokens) | copy-start | bytes 3145732
  130.7 1.1 copy-start
  131.8 1.0 copy-start.3
  132.8 9.7 %copy-start.2 = (bf16[32,16,1024]{2,1,0:T(8,128)(2,1)S(1)}, bf16[32,16,1024]{2,1,0:T(8,128)(2,1)}, u32[]{:S(2)}) copy-start(bf16[32,16,1024]{2,1,0:T(8,128)(2,1)} %copy-done.1) | copy-start | bytes 3145732
  132.8 32.6 %all-to-all-start.3 = ((bf16[32,16,1024]{2,1,0:T(8,128)(2,1)}), bf16[32,16,1024]{2,1,0:T(8,128)(2,1)S(1)}, u32[]{:S(2)}, u32[]{:S(2)}) async-start(bf16[32,16,1024]{2,1,0:T(8,128)(2,1)} %copy-done.3), calls=%async_computation.3 | async-start | bytes 2097152 | tf_op jit(solution)/shard_map/all_to_all | solution.py:122
  144.0 29.6 %collective-permute-start.3 = (bf16[896,512]{1,0:T(8,128)(2,1)S(1)}, bf16[896,512]{1,0:T(8,128)(2,1)}, u32[]{:S(2)}, u32[]{:S(2)}) collective-permute-start(bf16[896,512]{1,0:T(8,128)(2,1)S(1)} %convolution_convert_fusion), channel_id=1, source_target_pairs={{0,1},{1,0},{2,3},{3,2},{4,5},{5,4},{6,7},{7,6},{8,9},{9,8},{10,11... | collective-permute-start | bytes 2752520 | tf_op jit(solution)/shard_map/ppermute | solution.py:129
  165.6 10.6 %collective-permute-start.2 = (bf16[16,512]{1,0:T(8,128)(2,1)S(1)}, bf16[16,512]{1,0:T(8,128)(2,1)S(1)}, u32[]{:S(2)}, u32[]{:S(2)}) collective-permute-start(bf16[16,512]{1,0:T(8,128)(2,1)S(1)} %slice.33), channel_id=1, source_target_pairs={{0,1},{1,0},{2,3},{3,2},{4,5},{5,4},{6,7},{7,6},{8,9},{9,8},{10,11... | collective-permute-start | bytes 49160 | tf_op jit(solution)/shard_map/ppermute | solution.py:134

commit v2 on v1

v2 whole, which is shorter than its diff:
```python
import jax
import jax.numpy as jnp
from jax import lax
from jax.experimental import pallas as pl
from jax.experimental.pallas import tpu as pltpu
from jax.sharding import Mesh
from jax.sharding import PartitionSpec as P

BLOCK = 128
X_CHIPS = 4
SWAP = [(0, 1), (1, 0)]
NT = (((1,), (1,)), ((), ()))
TN = (((0,), (0,)), ((), ()))
F32 = jnp.float32
BF16 = jnp.bfloat16


def call(kernel, name, outs, args, smem=(), flops=0, moved=0):
    vmem = pl.BlockSpec(memory_space=pltpu.VMEM)
    scalar = pl.BlockSpec(memory_space=pltpu.SMEM)
    return pl.pallas_call(
        kernel,
        name=name,
        out_shape=outs,
        in_specs=[scalar if i in smem else vmem for i in range(len(args))],
        out_specs=jax.tree.map(lambda _: vmem, outs),
        cost_estimate=pl.CostEstimate(flops=flops, bytes_accessed=moved, transcendentals=0),
        compiler_params=pltpu.CompilerParams(vmem_limit_bytes=32 * 1024 * 1024),
    )(*args)


def dequant_kernel(scale, mant, out):
    mats, rows, cols = mant.shape
    for m in range(mats):
        for r in range(rows // BLOCK):
            for c in range(cols // BLOCK):
                at = (m, pl.ds(r * BLOCK, BLOCK), pl.ds(c * BLOCK, BLOCK))
                out[at] = (mant[at].astype(F32) * scale[m, r, c]).astype(BF16)


def gather_kernel(used, tokens, cotangent, out):
    rows, half = tokens.shape
    mine = rows // 2
    x, dy = tokens[...].astype(F32), cotangent[...].astype(F32)
    for c in range(2):
        at = slice(c * mine, (c + 1) * mine)
        block = jnp.concatenate([x[at], dy[at]], axis=0).astype(BF16)
        counts = used[at].astype(F32)
        tail = jnp.broadcast_to(jnp.concatenate([counts, counts], axis=0), (rows, BLOCK)).astype(BF16)
        for i in range(c, out.shape[0], 2):
            out[i, :, :half] = block
            out[i, :, half:] = tail


def spread_kernel(place, near, out):
    copies, chips, _, width = out.shape
    half = width // 2
    for i in range(chips):
        own = near[2 * i + place[0], :, :half].astype(F32)
        other = near[2 * i + 1 - place[0], :, :half].astype(F32)
        limit = near[2 * i, :, half:].astype(F32)[:, :1]
        for x in range(copies):
            keep = (place[1] * copies + x).astype(F32) < limit
            out[x, i, :, :half] = jnp.where(keep, own, 0.0).astype(BF16)
            out[x, i, :, half:] = jnp.where(keep, other, 0.0).astype(BF16)


def project_kernel(part, tokens, own, other, dy_out, keep, top, low):
    senders, rows, width = tokens.shape
    some = senders // 2
    half = width // 2
    units = own.shape[1]
    groups, chunk = keep.shape[:2]

    def split(h):
        wide = tokens[pl.ds(h * some, some)].astype(F32).reshape(some, 2, rows // 2, width)
        return [wide[:, i].reshape(-1, width) for i in range(2)]

    near, far = split(part[0]), split(1 - part[0])
    x, dy = [jnp.concatenate([far[i], near[i]], axis=0).astype(BF16) for i in range(2)]
    dy_out[...] = dy
    for m, left in ((0, x), (1, x), (2, dy)):
        term = lax.dot_general(left[:, :half], own[m], NT, preferred_element_type=F32)
        term += lax.dot_general(left[:, half:], other[m], NT, preferred_element_type=F32)
        term = term.astype(BF16).reshape(2 * groups, chunk, units)
        at = slice(m * units, (m + 1) * units)
        top[:, :, at] = term[:groups, : chunk // 2]
        low[:, :, at] = term[:groups, chunk // 2 :]
        keep[:, :, at] = term[groups:]


def activate_kernel(parts, out):
    copies, _, three = parts.shape
    units = three // 3
    total = jnp.sum(parts[...].astype(F32), axis=0)
    gate, up, dh = total[:, :units], total[:, units : 2 * units], total[:, 2 * units :]
    sig = jax.nn.sigmoid(gate)
    silu = gate * sig
    hidden = (silu * up).astype(BF16)
    dgate = (dh * up * sig * (1.0 + gate * (1.0 - sig))).astype(BF16)
    dup = (dh * silu).astype(BF16)
    for i in range(copies):
        out[i, :, :units] = hidden
        out[i, :, units : 2 * units] = dgate
        out[i, :, 2 * units :] = dup


def expand_kernel(part, acts, top, low, own, other, out, hidden_out):
    units = own.shape[1]
    owners, rows, width = out.shape
    some = owners // 2
    half = width // 2
    tokens = hidden_out.shape[0] // 2
    far = jnp.concatenate([top[...], low[...]], axis=1)
    for i, (h, left) in enumerate(((1 - part[0], far), (part[0], acts[...]))):
        left = left.reshape(tokens, 3 * units)
        hidden, dgate, dup = left[:, :units], left[:, units : 2 * units], left[:, 2 * units :]
        hidden_out[i * tokens : (i + 1) * tokens] = hidden
        for start, w in ((0, own), (half, other)):
            mixed = jnp.dot(hidden, w[2], preferred_element_type=F32)
            grad = jnp.dot(dgate, w[0], preferred_element_type=F32)
            grad += jnp.dot(dup, w[1], preferred_element_type=F32)
            both = jnp.concatenate(
                [mixed.reshape(some, rows // 2, half), grad.reshape(some, rows // 2, half)], axis=1
            )
            out[pl.ds(h * some, some), :, start : start + half] = both.astype(BF16)


def by_core(core, a, b):
    return jnp.where(core == 0, a, b), jnp.where(core == 0, b, a)


def body(tokens, cotangent, token_class, class_bands, mantissas, exponents):
    zs, xs, ks = lax.axis_size("z"), lax.axis_size("x"), lax.axis_size("k")
    lines = 2 * ks
    core = lax.axis_index("c")
    odd = lax.axis_index("p").reshape(1)
    rows, half = tokens.shape
    mine = rows // 2
    mats, units = mantissas.shape[:2]
    bands = zs * xs
    count = bands * mine
    chunk = count // lines
    left_pairs = [(i, i ^ 1) for i in range(lines)]
    right_pairs = [(i, (i + 1 if i % 2 else i - 1) % lines) for i in range(lines)]

    def swap_near(top, low):
        return (lax.ppermute(top, ("k", "p"), left_pairs), lax.ppermute(low, ("k", "p"), right_pairs))

    lookup = token_class[:, None] == jnp.arange(class_bands.shape[0], dtype=jnp.int32)[None, :]
    used = jnp.sum(jnp.where(lookup, class_bands[None, :], 0), axis=1, keepdims=True)
    pair = call(gather_kernel, "gather", jax.ShapeDtypeStruct((zs * 2, rows, half + BLOCK), BF16),
                (used, tokens, cotangent), moved=1 << 18)
    pair, mantissas, exponents = lax.optimization_barrier((pair, mantissas, exponents))
    near = lax.all_to_all(pair, ("z", "c"), 0, 0, tiled=True)

    raw_other, exponents_other = lax.ppermute(mantissas, "c", SWAP), lax.ppermute(exponents, "c", SWAP)

    def dequant(raw, powers, name):
        scale = jnp.exp2(powers.astype(F32)).astype(BF16).astype(F32)
        return call(dequant_kernel, name, jax.ShapeDtypeStruct(raw.shape, BF16), (scale, raw),
                    smem=(0,), flops=raw.size, moved=4 * raw.size)

    own = dequant(mantissas, exponents, "dequant_own")
    other = dequant(raw_other, exponents_other, "dequant_other")

    place = jnp.stack([core, lax.axis_index("z")])
    near, own, other, odd, place = lax.optimization_barrier((near, own, other, odd, place))
    masked = call(spread_kernel, "spread", jax.ShapeDtypeStruct((xs, zs, rows, 2 * half), BF16), (place, near),
                  smem=(0,), moved=2 << 20)
    gathered = lax.all_to_all(masked, "x", 0, 0, tiled=True).reshape(bands, rows, 2 * half)

    work = count * mats * units * 2 * half

    def shape(*dims):
        return jax.ShapeDtypeStruct(dims, BF16)

    wide = mats * units
    dy, keep, *send = call(
        project_kernel, "project",
        (shape(count, 2 * half), shape(ks, chunk, wide)) + (shape(ks, chunk // 2, wide),) * 2,
        (odd, gathered, own, other), smem=(0,), flops=2 * work, moved=10 << 20)
    got = jnp.concatenate(swap_near(*send), axis=1)
    parts = (keep.astype(F32) + got.astype(F32)).astype(BF16)
    parts = lax.all_to_all(parts, "k", 0, 0, tiled=True)
    acts = call(activate_kernel, "activate", shape(*parts.shape), (parts,), flops=parts.size, moved=4 * parts.size)
    acts = lax.all_to_all(acts, "k", 0, 0, tiled=True)
    top, low = swap_near(acts[:, : chunk // 2], acts[:, chunk // 2 :])
    terms, hidden = call(expand_kernel, "expand", (shape(bands, rows, 2 * half), shape(count, units)),
                         (odd, acts, top, low, own, other), smem=(0,), flops=2 * work, moved=10 << 20)

    terms = lax.all_to_all(terms.reshape(xs, zs, rows, 2 * half), "x", 0, 0, tiled=True)
    terms = jnp.sum(terms.astype(F32), axis=0).astype(BF16)
    here, away = by_core(core, terms[:, :, :half], terms[:, :, half:])
    terms = jnp.stack([here, away], axis=1).reshape(zs * 2, rows, half)
    terms = lax.all_to_all(terms, ("z", "c"), 0, 0, tiled=True).reshape(zs, 2, rows, half)
    total = jnp.sum(terms.astype(F32), axis=0).astype(BF16)
    mixed = total[:, :mine].reshape(rows, half)
    input_grad = total[:, mine:].reshape(rows, half)

    norm_factor = 1.0 / jnp.sqrt(jnp.float32(2 * count))
    down = lax.dot_general(hidden, dy[:, :half], TN, preferred_element_type=F32)
    away = lax.dot_general(hidden, dy[:, half:], TN, preferred_element_type=F32).astype(BF16)
    away = lax.ppermute(away, "c", SWAP)
    down_grad = ((down + away.astype(F32)) * norm_factor).astype(BF16)
    return mixed, input_grad, down_grad


def solution(mesh):
    dp, tensor = mesh.devices.shape
    split = Mesh(mesh.devices.reshape(dp // X_CHIPS, X_CHIPS, tensor // 4, 2, 2), ("z", "x", "k", "p", "c"))
    toks, cols = ("z", "x"), ("k", "p", "c")
    in_specs = (
        P(toks, cols),
        P(toks, cols),
        P(toks),
        P(),
        P(None, toks, cols),
        P(None, toks, cols),
    )
    out_specs = (P(toks, cols), P(toks, cols), P(toks, cols))
    return jax.shard_map(body, mesh=split, in_specs=in_specs, out_specs=out_specs, check_vma=False)
```

time: 178 us -> 163 us (0.916)
  blocking collectives: 106 us -> 61.6 us
  starting transfers between devices: 34.6 us -> 51.4 us
  waiting for transfers between devices: 15.2 us -> 26.7 us
    all_to_all x3, blocking collectives: 106 us -> 61.6 us  [the longest x1 23.1 us: body(): parts = lax.all_to_all(parts, 'k', 0, 0, tiled=True)]
    ppermute x3 -> x6, waiting for transfers between devices: 0.01 us -> 13.6 us  [the longest x2 10.1 us: swap_near(): lax.ppermute(low, ('k', 'p'), right_pairs)]
    all_to_all x1 -> x3, starting transfers between devices: 9.68 us -> 20 us  [the longest x1 11.3 us: body(): lax.all_to_all(terms, ('z', 'c'), 0, 0, tiled=True)]
    ppermute x3 -> x6, starting transfers between devices: 18.8 us -> 22.7 us  [the longest x1 8.78 us: body(): lax.ppermute(mantissas, 'c', SWAP)]
    ppermute x1, starting transfers between devices: 6.17 us -> 8.71 us  [body(): away = lax.ppermute(away, 'c', SWAP)]
    all_to_all x1 -> x3, waiting for transfers between devices: 15.2 us -> 13 us  [the longest x1 9.32 us: body(): lax.all_to_all(terms, ('z', 'c'), 0, 0, tiled=True)]
    unnamed x15 -> x16, local copies, waits for them, and re-layouts: 4.64 us -> 5.74 us
    pallas_call x4 -> x7, Pallas kernels: 9.07 us -> 8.91 us  [call(): pl.pallas_call(kernel, name=name, out_shape=outs, in_specs=[scalar if i i...]
  transfers between devices with their start and end apart: 5 -> 10, of which waited for: 1 -> 7; matrix products, arithmetic and copies ran while one was open for 3% -> 3% of each run, Pallas kernels for 1% -> 2%
where the time goes in v2:
time: 163 us; the launch traced here: 162 us
  blocking collectives  61.6 us (38%)
  starting transfers between devices  51.4 us (32%)
  waiting for transfers between devices  26.7 us (16%)
  Pallas kernels  8.91 us (5%)
  local copies, waits for them, and re-layouts  7.28 us (4%)
  matrix products  2.96 us (2%)
  other arithmetic  2 us (1%)
    all_to_all x1, blocking collectives, body(): parts = lax.all_to_all(parts, 'k', 0, 0, tiled=True)  23.1 us
    all_to_all x1, blocking collectives, body(): lax.all_to_all(masked, 'x', 0, 0, tiled=True).reshape(bands, rows, 2 * half)  19.4 us
    all_to_all x1, blocking collectives, body(): acts = lax.all_to_all(acts, 'k', 0, 0, tiled=True)  19.1 us
    all_to_all x1, starting transfers between devices, body(): lax.all_to_all(terms, ('z', 'c'), 0, 0, tiled=True)  11.3 us
    ppermute x2, waiting for transfers between devices, swap_near(): lax.ppermute(low, ('k', 'p'), right_pairs)  10.1 us
    all_to_all x1, waiting for transfers between devices, body(): lax.all_to_all(terms, ('z', 'c'), 0, 0, tiled=True)  9.32 us
    pallas_call x7, Pallas kernels, call(): pl.pallas_call(kernel, name=name, out_shape=outs, in_specs=[scalar if i i...  8.91 us
    ppermute x1, starting transfers between devices, body(): lax.ppermute(mantissas, 'c', SWAP)  8.78 us
  transfers between devices with their start and end apart: 10, of which 7 were waited for; matrix products, arithmetic and copies ran while one was open for 3% of the time, Pallas kernels for 2%

profile of v2, /device:TPU:1, one launch (start us, length us, event | category | flops | bytes accessed | tf_op | source)
XLA Modules:
  0.0 161.7 jit_solution(3886053079598038597)
XLA Ops:
  0.6 0.8 select_reduce_fusion
  1.4 0.1 copy.16.used
  1.5 0.7 copy-done.6
  2.2 0.7 copy-done.7
  2.9 0.8 gather.1
  3.7 8.8 %collective-permute-start.1 = (bf16[3,896,512]{2,1,0:T(8,128)(2,1)}, bf16[3,896,512]{2,1,0:T(8,128)(2,1)}, u32[]{:S(2)}, u32[]{:S(2)}) collective-permute-start(bf16[3,896,512]{2,1,0:T(8,128)(2,1)} %mant), channel_id=1, source_target_pairs={{0,1},{1,0},{2,3},{3,2},{4,5},{5,4},{6,7},{7,6},{8,9},{9,8},{10,11... | collective-permute-start | bytes 8257544 | tf_op jit(solution)/shard_map/ppermute | solution.py:157
  12.5 5.1 %all-to-all-start = ((bf16[16,16,640]{2,1,0:T(8,128)(2,1)}), bf16[16,16,640]{2,1,0:T(8,128)(2,1)S(1)}, u32[]{:S(2)}, u32[]{:S(2)}) async-start(bf16[16,16,640]{2,1,0:T(8,128)(2,1)} %gather.1), calls=%async_computation | async-start | bytes 655360 | tf_op jit(solution)/shard_map/all_to_all | solution.py:155
  17.6 0.8 copy.17
  18.4 2.0 %collective-permute-start = (s32[3,7,4]{2,1,0:T(8,128)S(1)}, s32[3,7,4]{2,1,0:T(8,128)S(1)}, u32[]{:S(2)}, u32[]{:S(2)}) collective-permute-start(s32[3,7,4]{2,1,0:T(8,128)S(1)} %copy.17), channel_id=1, source_target_pairs={{0,1},{1,0},{2,3},{3,2},{4,5},{5,4},{6,7},{7,6},{8,9},{9,8},{10,11... | collective-permute-start | bytes 1016 | tf_op jit(solution)/shard_map/ppermute | solution.py:157
  20.4 0.1 pad_add_fusion.place
  20.5 1.8 %copy-done.2 = bf16[3,896,512]{2,1,0:T(8,128)(2,1)S(1)} copy-done((bf16[3,896,512]{2,1,0:T(8,128)(2,1)S(1)}, bf16[3,896,512]{2,1,0:T(8,128)(2,1)}, u32[]{:S(2)}) %copy-start.2) | copy-done | bytes 2752536
  22.3 1.3 dequant_own.1.own
  23.5 0.0 collective-permute-done
  23.6 0.0 collective-permute-done.1.mant
  23.6 2.3 %dequant_other.1.other = bf16[3,896,512]{2,1,0:T(8,128)(2,1)S(1)} custom-call(f32[3,7,4]{2,1,0:T(8,128)S(1)} %fusion.3.scale, bf16[3,896,512]{2,1,0:T(8,128)(2,1)} %collective-permute-done.1.mant), custom_call_target="tpu_custom_call" | custom-call | flops 1376256 | bytes 5505024 | tf_op jit(solution)/shard_map/dequant_other/pallas_call | solution.py:21
  25.9 0.0 copy-start
  25.9 1.5 copy-done
  27.5 3.2 %all-to-all-done.near = bf16[16,16,640]{2,1,0:T(8,128)(2,1)S(1)} async-done(((bf16[16,16,640]{2,1,0:T(8,128)(2,1)}), bf16[16,16,640]{2,1,0:T(8,128)(2,1)S(1)}, u32[]{:S(2)}, u32[]{:S(2)}) %all-to-all-start) | async-done | bytes 327712 | tf_op jit(solution)/shard_map/all_to_all | solution.py:155
  30.7 0.7 spread.1
  31.4 19.4 %all_to_all.30 = bf16[4,8,16,1024]{3,2,1,0:T(8,128)(2,1)S(1)} all-to-all(bf16[4,8,16,1024]{3,2,1,0:T(8,128)(2,1)S(1)} %spread.1), channel_id=1, replica_groups=mesh['z'=8,'x'=4,'k'=4,'p'=2,'c'=2] {'x'}, dimensions={0} | all-to-all | bytes 2097152 | tf_op jit(solution)/shard_map/all_to_all | solution.py:171
  50.8 1.8 %project.1 = (bf16[256,1024]{1,0:T(8,128)(2,1)S(1)}, bf16[4,32,2688]{2,1,0:T(8,128)(2,1)S(1)}, bf16[4,16,2688]{2,1,0:T(8,128)(2,1)S(1)}, bf16[4,16,2688]{2,1,0:T(8,128)(2,1)S(1)}) custom-call(s32[1]{0:T(128)} %bitcast.1.part, bf16[32,16,1024]{2,1,0:T(8,128)(2,1)S(1)} %bitcast.20, bf16[3,896,512]{2,1,0:T(8,128)(2,1)S(1)} %dequant_own.1.own, ...), custom_call_target="tpu_custom_call" | custom-call | flops 1409286144 | bytes 10485760 | tf_op jit(solution)/shard_map/project/pallas_call | solution.py:21
  52.6 0.0 copy-start.4
  52.7 3.2 %collective-permute-start.2 = (bf16[4,16,2688]{2,1,0:T(8,128)(2,1)S(1)}, bf16[4,16,2688]{2,1,0:T(8,128)(2,1)S(1)}, u32[]{:S(2)}, u32[]{:S(2)}) collective-permute-start(bf16[4,16,2688]{2,1,0:T(8,128)(2,1)S(1)} %get-tuple-element.26), channel_id=1, source_target_pairs={{0,2},{2,0},{4,6},{6,4},{8,10},{10,8},{12,14},{14,12},{1,3},{3,1},... | collective-permute-start | bytes 1032200 | tf_op jit(solution)/shard_map/ppermute | solution.py:148
  55.9 4.9 %collective-permute-start.3 = (bf16[4,16,2688]{2,1,0:T(8,128)(2,1)S(1)}, bf16[4,16,2688]{2,1,0:T(8,128)(2,1)S(1)}, u32[]{:S(2)}, u32[]{:S(2)}) collective-permute-start(bf16[4,16,2688]{2,1,0:T(8,128)(2,1)S(1)} %get-tuple-element.27), channel_id=1, source_target_pairs={{0,14},{2,4},{4,2},{6,8},{8,6},{10,12},{12,10},{14,0},{1,15},{3,5}... | collective-permute-start | bytes 1032200 | tf_op jit(solution)/shard_map/ppermute | solution.py:148
  60.8 2.9 %collective-permute-done.2 = bf16[4,16,2688]{2,1,0:T(8,128)(2,1)S(1)} collective-permute-done((bf16[4,16,2688]{2,1,0:T(8,128)(2,1)S(1)}, bf16[4,16,2688]{2,1,0:T(8,128)(2,1)S(1)}, u32[]{:S(2)}, u32[]{:S(2)}) %collective-permute-start.2) | collective-permute-done | bytes 344096 | tf_op jit(solution)/shard_map/ppermute | solution.py:148
  63.6 4.7 %collective-permute-done.3 = bf16[4,16,2688]{2,1,0:T(8,128)(2,1)S(1)} collective-permute-done((bf16[4,16,2688]{2,1,0:T(8,128)(2,1)S(1)}, bf16[4,16,2688]{2,1,0:T(8,128)(2,1)S(1)}, u32[]{:S(2)}, u32[]{:S(2)}) %collective-permute-start.3) | collective-permute-done | bytes 344096 | tf_op jit(solution)/shard_map/ppermute | solution.py:148
  68.3 0.2 add_convert_fusion
  68.5 23.1 %all_to_all.31.parts = bf16[4,32,2688]{2,1,0:T(8,128)(2,1)S(1)} all-to-all(bf16[4,32,2688]{2,1,0:T(8,128)(2,1)S(1)} %add_convert_fusion), channel_id=1, replica_groups=mesh['z'=8,'x'=4,'k'=4,'p'=2,'c'=2] {'k'}, dimensions={0} | all-to-all | bytes 1376256 | tf_op jit(solution)/shard_map/all_to_all | solution.py:185
  91.6 0.1 activate.1
  91.7 0.0 copy-done.4
  91.7 19.1 %all_to_all.32.acts = bf16[4,32,2688]{2,1,0:T(8,128)(2,1)S(1)} all-to-all(bf16[4,32,2688]{2,1,0:T(8,128)(2,1)S(1)} %activate.1), channel_id=1, replica_groups=mesh['z'=8,'x'=4,'k'=4,'p'=2,'c'=2] {'k'}, dimensions={0} | all-to-all | bytes 1376256 | tf_op jit(solution)/shard_map/all_to_all | solution.py:187
  110.9 1.9 %collective-permute-start.5 = (bf16[4,16,2688]{2,1,0:T(8,128)(2,1)S(1)}, bf16[4,16,2688]{2,1,0:T(8,128)(2,1)S(1)}, u32[]{:S(2)}, u32[]{:S(2)}) collective-permute-start(bf16[4,16,2688]{2,1,0:T(8,128)(2,1)S(1)} %get-tuple-element.31), channel_id=1, source_target_pairs={{0,14},{2,4},{4,2},{6,8},{8,6},{10,12},{12,10},{14,0},{1,15},{3,5}... | collective-permute-start | bytes 1032200 | tf_op jit(solution)/shard_map/ppermute | solution.py:148
  112.8 1.9 %collective-permute-start.4 = (bf16[4,16,2688]{2,1,0:T(8,128)(2,1)S(1)}, bf16[4,16,2688]{2,1,0:T(8,128)(2,1)S(1)}, u32[]{:S(2)}, u32[]{:S(2)}) collective-permute-start(bf16[4,16,2688]{2,1,0:T(8,128)(2,1)S(1)} %get-tuple-element.32), channel_id=1, source_target_pairs={{0,2},{2,0},{4,6},{6,4},{8,10},{10,8},{12,14},{14,12},{1,3},{3,1},... | collective-permute-start | bytes 1032200 | tf_op jit(solution)/shard_map/ppermute | solution.py:148
  114.7 5.3 %collective-permute-done.5.low = bf16[4,16,2688]{2,1,0:T(8,128)(2,1)S(1)} collective-permute-done((bf16[4,16,2688]{2,1,0:T(8,128)(2,1)S(1)}, bf16[4,16,2688]{2,1,0:T(8,128)(2,1)S(1)}, u32[]{:S(2)}, u32[]{:S(2)}) %collective-permute-start.5) | collective-permute-done | bytes 344096 | tf_op jit(solution)/shard_map/ppermute | solution.py:148
  120.1 0.7 collective-permute-done.4.top
  120.8 1.8 %expand.1 = (bf16[32,16,1024]{2,1,0:T(8,128)(2,1)S(1)}, bf16[256,896]{1,0:T(8,128)(2,1)S(1)}) custom-call(s32[1]{0:T(128)} %bitcast.1.part, bf16[4,32,2688]{2,1,0:T(8,128)(2,1)S(1)} %all_to_all.32.acts, bf16[4,16,2688]{2,1,0:T(8,128)(2,1)S(1)} %collective-permute-done.4.top, bf16[4,16,2688]{2,1,0:T(8,128)(2,1)S(1)} %collective-permute-done.5.low, ...), custom_call_target="tpu_custom_call" | custom-call | flops 1409286144 | bytes 10485760 | tf_op jit(solution)/shard_map/expand/pallas_call | solution.py:21
  122.6 1.0 copy-done.3
  123.6 3.6 %all-to-all-start.4 = ((bf16[4,8,16,1024]{3,2,1,0:T(8,128)(2,1)}), bf16[4,8,16,1024]{3,2,1,0:T(8,128)(2,1)S(1)}, u32[]{:S(2)}, u32[]{:S(2)}) async-start(bf16[4,8,16,1024]{3,2,1,0:T(8,128)(2,1)} %bitcast.21), calls=%async_computation.4 | async-start | bytes 2097152 | tf_op jit(solution)/shard_map/all_to_all | solution.py:192
  127.3 0.4 convolution_convert_fusion
  127.7 8.7 %collective-permute-start.6 = (bf16[896,512]{1,0:T(8,128)(2,1)S(1)}, bf16[896,512]{1,0:T(8,128)(2,1)}, u32[]{:S(2)}, u32[]{:S(2)}) collective-permute-start(bf16[896,512]{1,0:T(8,128)(2,1)S(1)} %convolution_convert_fusion), channel_id=1, source_target_pairs={{0,1},{1,0},{2,3},{3,2},{4,5},{5,4},{6,7},{7,6},{8,9},{9,8},{10,11... | collective-permute-start | bytes 2752520 | tf_op jit(solution)/shard_map/ppermute | solution.py:204
  136.4 0.5 all-to-all-done.4
  137.0 0.2 reduce_sum.34
  137.2 0.7 pad_maximum_fusion
  137.9 11.3 %all-to-all-start.5 = ((bf16[16,16,512]{2,1,0:T(8,128)(2,1)}), bf16[16,16,512]{2,1,0:T(8,128)(2,1)S(1)}, u32[]{:S(2)}, u32[]{:S(2)}) async-start(bf16[16,16,512]{2,1,0:T(8,128)(2,1)} %bitcast.9), calls=%async_computation.5 | async-start | bytes 524288 | tf_op jit(solution)/shard_map/all_to_all | solution.py:196
  149.2 0.0 collective-permute-done.6
  149.2 2.5 %multiply_convert_fusion = bf16[896,512]{1,0:T(8,128)(2,1)} fusion(bf16[896,512]{1,0:T(8,128)(2,1)} %collective-permute-done.6, bf16[256,896]{1,0:T(8,128)(2,1)S(1)} %get-tuple-element.29, bf16[256,1024]{1,0:T(8,128)(2,1)S(1)} %copy-done.5), kind=kOutput, calls=%fused_computation | convolution fusion | flops 236716032 | bytes 2555904 | tf_op jit(solution)/shard_map/dot_general | solution.py:202
  151.7 9.3 %all-to-all-done.5 = bf16[16,16,512]{2,1,0:T(8,128)(2,1)S(1)} async-done(((bf16[16,16,512]{2,1,0:T(8,128)(2,1)}), bf16[16,16,512]{2,1,0:T(8,128)(2,1)S(1)}, u32[]{:S(2)}, u32[]{:S(2)}) %all-to-all-start.5) | async-done | bytes 262176 | tf_op jit(solution)/shard_map/all_to_all | solution.py:196
  161.1 0.6 slice_bitcast_fusion
  (13 shorter events, 0.1 us)
Async XLA Ops:
  1.5 0.7 copy-start.6
  2.2 0.7 copy-start.7
  3.7 19.9 %collective-permute-start.1 = (bf16[3,896,512]{2,1,0:T(8,128)(2,1)}, bf16[3,896,512]{2,1,0:T(8,128)(2,1)}, u32[]{:S(2)}, u32[]{:S(2)}) collective-permute-start(bf16[3,896,512]{2,1,0:T(8,128)(2,1)} %mant), channel_id=1, source_target_pairs={{0,1},{1,0},{2,3},{3,2},{4,5},{5,4},{6,7},{7,6},{8,9},{9,8},{10,11... | collective-permute-start | bytes 8257544 | tf_op jit(solution)/shard_map/ppermute | solution.py:157
  12.5 18.1 %all-to-all-start = ((bf16[16,16,640]{2,1,0:T(8,128)(2,1)}), bf16[16,16,640]{2,1,0:T(8,128)(2,1)S(1)}, u32[]{:S(2)}, u32[]{:S(2)}) async-start(bf16[16,16,640]{2,1,0:T(8,128)(2,1)} %gather.1), calls=%async_computation | async-start | bytes 655360 | tf_op jit(solution)/shard_map/all_to_all | solution.py:155
  18.4 5.2 %collective-permute-start = (s32[3,7,4]{2,1,0:T(8,128)S(1)}, s32[3,7,4]{2,1,0:T(8,128)S(1)}, u32[]{:S(2)}, u32[]{:S(2)}) collective-permute-start(s32[3,7,4]{2,1,0:T(8,128)S(1)} %copy.17), channel_id=1, source_target_pairs={{0,1},{1,0},{2,3},{3,2},{4,5},{5,4},{6,7},{7,6},{8,9},{9,8},{10,11... | collective-permute-start | bytes 1016 | tf_op jit(solution)/shard_map/ppermute | solution.py:157
  20.5 1.8 %copy-start.2 = (bf16[3,896,512]{2,1,0:T(8,128)(2,1)S(1)}, bf16[3,896,512]{2,1,0:T(8,128)(2,1)}, u32[]{:S(2)}) copy-start(bf16[3,896,512]{2,1,0:T(8,128)(2,1)} %mant) | copy-start | bytes 8257540
  25.9 1.5 copy-start
  30.7 20.2 %copy-start.1 = (bf16[3,896,512]{2,1,0:T(8,128)(2,1)S(1)}, bf16[3,896,512]{2,1,0:T(8,128)(2,1)}, u32[]{:S(2)}) copy-start(bf16[3,896,512]{2,1,0:T(8,128)(2,1)} %copy-done) | copy-start | bytes 8257540
  52.6 39.1 %copy-start.4 = (bf16[256,1024]{1,0:T(8,128)(2,1)}, bf16[256,1024]{1,0:T(8,128)(2,1)S(1)}, u32[]{:S(2)}) copy-start(bf16[256,1024]{1,0:T(8,128)(2,1)S(1)} %get-tuple-element.30) | copy-start | bytes 1572868
  52.7 10.9 %collective-permute-start.2 = (bf16[4,16,2688]{2,1,0:T(8,128)(2,1)S(1)}, bf16[4,16,2688]{2,1,0:T(8,128)(2,1)S(1)}, u32[]{:S(2)}, u32[]{:S(2)}) collective-permute-start(bf16[4,16,2688]{2,1,0:T(8,128)(2,1)S(1)} %get-tuple-element.26), channel_id=1, source_target_pairs={{0,2},{2,0},{4,6},{6,4},{8,10},{10,8},{12,14},{14,12},{1,3},{3,1},... | collective-permute-start | bytes 1032200 | tf_op jit(solution)/shard_map/ppermute | solution.py:148
  55.9 12.5 %collective-permute-start.3 = (bf16[4,16,2688]{2,1,0:T(8,128)(2,1)S(1)}, bf16[4,16,2688]{2,1,0:T(8,128)(2,1)S(1)}, u32[]{:S(2)}, u32[]{:S(2)}) collective-permute-start(bf16[4,16,2688]{2,1,0:T(8,128)(2,1)S(1)} %get-tuple-element.27), channel_id=1, source_target_pairs={{0,14},{2,4},{4,2},{6,8},{8,6},{10,12},{12,10},{14,0},{1,15},{3,5}... | collective-permute-start | bytes 1032200 | tf_op jit(solution)/shard_map/ppermute | solution.py:148
  110.9 9.2 %collective-permute-start.5 = (bf16[4,16,2688]{2,1,0:T(8,128)(2,1)S(1)}, bf16[4,16,2688]{2,1,0:T(8,128)(2,1)S(1)}, u32[]{:S(2)}, u32[]{:S(2)}) collective-permute-start(bf16[4,16,2688]{2,1,0:T(8,128)(2,1)S(1)} %get-tuple-element.31), channel_id=1, source_target_pairs={{0,14},{2,4},{4,2},{6,8},{8,6},{10,12},{12,10},{14,0},{1,15},{3,5}... | collective-permute-start | bytes 1032200 | tf_op jit(solution)/shard_map/ppermute | solution.py:148
  112.8 8.0 %collective-permute-start.4 = (bf16[4,16,2688]{2,1,0:T(8,128)(2,1)S(1)}, bf16[4,16,2688]{2,1,0:T(8,128)(2,1)S(1)}, u32[]{:S(2)}, u32[]{:S(2)}) collective-permute-start(bf16[4,16,2688]{2,1,0:T(8,128)(2,1)S(1)} %get-tuple-element.32), channel_id=1, source_target_pairs={{0,2},{2,0},{4,6},{6,4},{8,10},{10,8},{12,14},{14,12},{1,3},{3,1},... | collective-permute-start | bytes 1032200 | tf_op jit(solution)/shard_map/ppermute | solution.py:148
  122.6 1.0 copy-start.3
  123.6 3.7 %copy-start.5 = (bf16[256,1024]{1,0:T(8,128)(2,1)S(1)}, bf16[256,1024]{1,0:T(8,128)(2,1)}, u32[]{:S(2)}) copy-start(bf16[256,1024]{1,0:T(8,128)(2,1)} %copy-done.4) | copy-start | bytes 1572868
  123.6 13.4 %all-to-all-start.4 = ((bf16[4,8,16,1024]{3,2,1,0:T(8,128)(2,1)}), bf16[4,8,16,1024]{3,2,1,0:T(8,128)(2,1)S(1)}, u32[]{:S(2)}, u32[]{:S(2)}) async-start(bf16[4,8,16,1024]{3,2,1,0:T(8,128)(2,1)} %bitcast.21), calls=%async_computation.4 | async-start | bytes 2097152 | tf_op jit(solution)/shard_map/all_to_all | solution.py:192
  127.7 21.5 %collective-permute-start.6 = (bf16[896,512]{1,0:T(8,128)(2,1)S(1)}, bf16[896,512]{1,0:T(8,128)(2,1)}, u32[]{:S(2)}, u32[]{:S(2)}) collective-permute-start(bf16[896,512]{1,0:T(8,128)(2,1)S(1)} %convolution_convert_fusion), channel_id=1, source_target_pairs={{0,1},{1,0},{2,3},{3,2},{4,5},{5,4},{6,7},{7,6},{8,9},{9,8},{10,11... | collective-permute-start | bytes 2752520 | tf_op jit(solution)/shard_map/ppermute | solution.py:204
  137.9 23.1 %all-to-all-start.5 = ((bf16[16,16,512]{2,1,0:T(8,128)(2,1)}), bf16[16,16,512]{2,1,0:T(8,128)(2,1)S(1)}, u32[]{:S(2)}, u32[]{:S(2)}) async-start(bf16[16,16,512]{2,1,0:T(8,128)(2,1)} %bitcast.9), calls=%async_computation.5 | async-start | bytes 524288 | tf_op jit(solution)/shard_map/all_to_all | solution.py:196

commit v3 on v2

--- a/solution.py
+++ b/solution.py
@@ -38,20 +38,6 @@
                 out[at] = (mant[at].astype(F32) * scale[m, r, c]).astype(BF16)
 
 
-def gather_kernel(used, tokens, cotangent, out):
-    rows, half = tokens.shape
-    mine = rows // 2
-    x, dy = tokens[...].astype(F32), cotangent[...].astype(F32)
-    for c in range(2):
-        at = slice(c * mine, (c + 1) * mine)
-        block = jnp.concatenate([x[at], dy[at]], axis=0).astype(BF16)
-        counts = used[at].astype(F32)
-        tail = jnp.broadcast_to(jnp.concatenate([counts, counts], axis=0), (rows, BLOCK)).astype(BF16)
-        for i in range(c, out.shape[0], 2):
-            out[i, :, :half] = block
-            out[i, :, half:] = tail
-
-
 def spread_kernel(place, near, out):
     copies, chips, _, width = out.shape
     half = width // 2
@@ -65,12 +51,12 @@
             out[x, i, :, half:] = jnp.where(keep, other, 0.0).astype(BF16)
 
 
-def project_kernel(part, tokens, own, other, dy_out, keep, top, low):
+def project_kernel(part, tokens, own, other, dy_own, dy_other, keep, send):
     senders, rows, width = tokens.shape
     some = senders // 2
     half = width // 2
     units = own.shape[1]
-    groups, chunk = keep.shape[:2]
+    groups, chunk = keep.shape[0], keep.shape[1] // 3
 
     def split(h):
         wide = tokens[pl.ds(h * some, some)].astype(F32).reshape(some, 2, rows // 2, width)
@@ -78,31 +64,31 @@
 
     near, far = split(part[0]), split(1 - part[0])
     x, dy = [jnp.concatenate([far[i], near[i]], axis=0).astype(BF16) for i in range(2)]
-    dy_out[...] = dy
+    dy_own[...] = dy[:, :half]
+    dy_other[...] = dy[:, half:]
     for m, left in ((0, x), (1, x), (2, dy)):
         term = lax.dot_general(left[:, :half], own[m], NT, preferred_element_type=F32)
         term += lax.dot_general(left[:, half:], other[m], NT, preferred_element_type=F32)
         term = term.astype(BF16).reshape(2 * groups, chunk, units)
-        at = slice(m * units, (m + 1) * units)
-        top[:, :, at] = term[:groups, : chunk // 2]
-        low[:, :, at] = term[:groups, chunk // 2 :]
-        keep[:, :, at] = term[groups:]
+        at = slice(m * chunk, (m + 1) * chunk)
+        send[:, at] = term[:groups]
+        keep[:, at] = term[groups:]
 
 
 def activate_kernel(parts, out):
-    copies, _, three = parts.shape
-    units = three // 3
+    copies, three, _ = parts.shape
+    chunk = three // 3
     total = jnp.sum(parts[...].astype(F32), axis=0)
-    gate, up, dh = total[:, :units], total[:, units : 2 * units], total[:, 2 * units :]
+    gate, up, dh = total[:chunk], total[chunk : 2 * chunk], total[2 * chunk :]
     sig = jax.nn.sigmoid(gate)
     silu = gate * sig
     hidden = (silu * up).astype(BF16)
     dgate = (dh * up * sig * (1.0 + gate * (1.0 - sig))).astype(BF16)
     dup = (dh * silu).astype(BF16)
     for i in range(copies):
-        out[i, :, :units] = hidden
-        out[i, :, units : 2 * units] = dgate
-        out[i, :, 2 * units :] = dup
+        out[i, :chunk] = hidden
+        out[i, chunk : 2 * chunk] = dgate
+        out[i, 2 * chunk :] = dup
 
 
 def expand_kernel(part, acts, top, low, own, other, out, hidden_out):
@@ -111,10 +97,12 @@
     some = owners // 2
     half = width // 2
     tokens = hidden_out.shape[0] // 2
-    far = jnp.concatenate([top[...], low[...]], axis=1)
-    for i, (h, left) in enumerate(((1 - part[0], far), (part[0], acts[...]))):
-        left = left.reshape(tokens, 3 * units)
-        hidden, dgate, dup = left[:, :units], left[:, units : 2 * units], left[:, 2 * units :]
+    chunk = acts.shape[1] // 3
+    groups = top.shape[0]
+    for i, (h, parts) in enumerate(((1 - part[0], (top, low)), (part[0], (acts.at[:groups], acts.at[groups:])))):
+        hidden, dgate, dup = [
+            jnp.concatenate([p[:, j * chunk : (j + 1) * chunk].reshape(-1, units) for p in parts], axis=0) for j in range(3)
+        ]
         hidden_out[i * tokens : (i + 1) * tokens] = hidden
         for start, w in ((0, own), (half, other)):
             mixed = jnp.dot(hidden, w[2], preferred_element_type=F32)
@@ -126,8 +114,12 @@
             out[pl.ds(h * some, some), :, start : start + half] = both.astype(BF16)
 
 
-def by_core(core, a, b):
-    return jnp.where(core == 0, a, b), jnp.where(core == 0, b, a)
+def gather_sum_kernel(core, terms, out):
+    half = out.shape[2]
+    total = jnp.sum(terms[...].astype(F32), axis=0).astype(BF16)
+    for i in range(total.shape[0]):
+        out[2 * i + core[0]] = total[i, :, :half]
+        out[2 * i + 1 - core[0]] = total[i, :, half:]
 
 
 def body(tokens, cotangent, token_class, class_bands, mantissas, exponents):
@@ -144,13 +136,19 @@
     left_pairs = [(i, i ^ 1) for i in range(lines)]
     right_pairs = [(i, (i + 1 if i % 2 else i - 1) % lines) for i in range(lines)]
 
+    pairs = [
+        (2 * src + c, 2 * dst + c) for c, swaps in enumerate((left_pairs, right_pairs)) for src, dst in swaps
+    ]
+
     def swap_near(top, low):
         return (lax.ppermute(top, ("k", "p"), left_pairs), lax.ppermute(low, ("k", "p"), right_pairs))
 
     lookup = token_class[:, None] == jnp.arange(class_bands.shape[0], dtype=jnp.int32)[None, :]
-    used = jnp.sum(jnp.where(lookup, class_bands[None, :], 0), axis=1, keepdims=True)
-    pair = call(gather_kernel, "gather", jax.ShapeDtypeStruct((zs * 2, rows, half + BLOCK), BF16),
-                (used, tokens, cotangent), moved=1 << 18)
+    used = jnp.sum(jnp.where(lookup, class_bands[None, :], 0), axis=1).astype(BF16).reshape(2, mine, 1)
+    tail = jnp.broadcast_to(jnp.concatenate([used, used], axis=1), (2, rows, BLOCK))
+    pair = jnp.concatenate([tokens.reshape(2, mine, half), cotangent.reshape(2, mine, half)], axis=1)
+    pair = jnp.concatenate([pair, tail], axis=2)
+    pair = jnp.broadcast_to(pair[None], (zs, 2, rows, half + BLOCK)).reshape(zs * 2, rows, half + BLOCK)
     pair, mantissas, exponents = lax.optimization_barrier((pair, mantissas, exponents))
     near = lax.all_to_all(pair, ("z", "c"), 0, 0, tiled=True)
 
@@ -175,34 +173,31 @@
     def shape(*dims):
         return jax.ShapeDtypeStruct(dims, BF16)
 
-    wide = mats * units
-    dy, keep, *send = call(
-        project_kernel, "project",
-        (shape(count, 2 * half), shape(ks, chunk, wide)) + (shape(ks, chunk // 2, wide),) * 2,
+    dy_own, dy_other, keep, send = call(
+        project_kernel, "project", (shape(count, half),) * 2 + (shape(ks, 3 * chunk, units),) * 2,
         (odd, gathered, own, other), smem=(0,), flops=2 * work, moved=10 << 20)
-    got = jnp.concatenate(swap_near(*send), axis=1)
-    parts = (keep.astype(F32) + got.astype(F32)).astype(BF16)
+    parts = (keep.astype(F32) + lax.ppermute(send, ("k", "p", "c"), pairs).astype(F32)).astype(BF16)
     parts = lax.all_to_all(parts, "k", 0, 0, tiled=True)
     acts = call(activate_kernel, "activate", shape(*parts.shape), (parts,), flops=parts.size, moved=4 * parts.size)
     acts = lax.all_to_all(acts, "k", 0, 0, tiled=True)
-    top, low = swap_near(acts[:, : chunk // 2], acts[:, chunk // 2 :])
+    top, low = swap_near(acts[: ks // 2], acts[ks // 2 :])
     terms, hidden = call(expand_kernel, "expand", (shape(bands, rows, 2 * half), shape(count, units)),
                          (odd, acts, top, low, own, other), smem=(0,), flops=2 * work, moved=10 << 20)
 
     terms = lax.all_to_all(terms.reshape(xs, zs, rows, 2 * half), "x", 0, 0, tiled=True)
-    terms = jnp.sum(terms.astype(F32), axis=0).astype(BF16)
-    here, away = by_core(core, terms[:, :, :half], terms[:, :, half:])
-    terms = jnp.stack([here, away], axis=1).reshape(zs * 2, rows, half)
+    terms = call(gather_sum_kernel, "gather_sum", shape(zs * 2, rows, half), (core.reshape(1), terms),
+                 smem=(0,), moved=1 << 20)
+    terms, hidden, dy_other = lax.optimization_barrier((terms, hidden, dy_other))
     terms = lax.all_to_all(terms, ("z", "c"), 0, 0, tiled=True).reshape(zs, 2, rows, half)
     total = jnp.sum(terms.astype(F32), axis=0).astype(BF16)
     mixed = total[:, :mine].reshape(rows, half)
     input_grad = total[:, mine:].reshape(rows, half)
 
     norm_factor = 1.0 / jnp.sqrt(jnp.float32(2 * count))
-    down = lax.dot_general(hidden, dy[:, :half], TN, preferred_element_type=F32)
-    away = lax.dot_general(hidden, dy[:, half:], TN, preferred_element_type=F32).astype(BF16)
-    away = lax.ppermute(away, "c", SWAP)
-    down_grad = ((down + away.astype(F32)) * norm_factor).astype(BF16)
+    dy_got, got = lax.ppermute(dy_other, "c", SWAP), lax.ppermute(hidden, "c", SWAP)
+    down = lax.dot_general(jnp.concatenate([hidden, got]), jnp.concatenate([dy_own, dy_got]), TN,
+                           preferred_element_type=F32)
+    down_grad = (down * norm_factor).astype(BF16)
     return mixed, input_grad, down_grad
 
 

time: 163 us -> 161 us (0.988)
  blocking collectives: 61.6 us -> 75.8 us
  starting transfers between devices: 51.4 us -> 39.2 us
    all_to_all x0 -> x1, blocking collectives: none -> 12.3 us  [body(): lax.all_to_all(terms.reshape(xs, zs, rows, 2 * half), 'x', 0, 0, tiled=True)]
    ppermute x1 -> x3, waiting for transfers between devices: 0.01 us -> 9.72 us  [the longest x1 8.31 us: body(): lax.ppermute(send, ('k', 'p', 'c'), pairs).astype(F32)]
    all_to_all x1, starting transfers between devices: 11.3 us -> 3.82 us  [body(): lax.all_to_all(terms, ('z', 'c'), 0, 0, tiled=True)]
    ppermute x1 -> x3, starting transfers between devices: 8.71 us -> 15.7 us  [the longest x1 8.6 us: body(): lax.ppermute(hidden, 'c', SWAP)]
    ppermute x2 -> x1, starting transfers between devices: 6.79 us -> 1.92 us  [swap_near(): lax.ppermute(low, ('k', 'p'), right_pairs)]
    ppermute x2 -> x1, waiting for transfers between devices: 10.1 us -> 5.35 us  [swap_near(): lax.ppermute(low, ('k', 'p'), right_pairs)]
    all_to_all x1 -> x0, starting transfers between devices: 3.65 us -> none  [body(): lax.all_to_all(terms.reshape(xs, zs, rows, 2 * half), 'x', 0, 0, tiled=True)]
    ppermute x2 -> x1, starting transfers between devices: 5.13 us -> 1.92 us  [swap_near(): lax.ppermute(top, ('k', 'p'), left_pairs)]
  transfers between devices with their start and end apart: 10 -> 9, of which waited for: 7 -> 6; matrix products, arithmetic and copies ran while one was open for 3% -> 2% of each run, Pallas kernels for 2% -> 2%
where the time goes in v3:
time: 161 us; the launch traced here: 160 us
  blocking collectives  75.8 us (47%)
  starting transfers between devices  39.2 us (24%)
  waiting for transfers between devices  25.7 us (16%)
  Pallas kernels  8.97 us (6%)
  local copies, waits for them, and re-layouts  5.7 us (4%)
  other arithmetic  1.89 us (1%)
    all_to_all x1, blocking collectives, body(): parts = lax.all_to_all(parts, 'k', 0, 0, tiled=True)  25.1 us
    all_to_all x1, blocking collectives, body(): lax.all_to_all(masked, 'x', 0, 0, tiled=True).reshape(bands, rows, 2 * half)  19.4 us
    all_to_all x1, blocking collectives, body(): acts = lax.all_to_all(acts, 'k', 0, 0, tiled=True)  19 us
    all_to_all x1, blocking collectives, body(): lax.all_to_all(terms.reshape(xs, zs, rows, 2 * half), 'x', 0, 0, tiled=True)  12.3 us
    pallas_call x7, Pallas kernels, call(): pl.pallas_call(kernel, name=name, out_shape=outs, in_specs=[scalar if i i...  8.97 us
    ppermute x1, starting transfers between devices, body(): lax.ppermute(mantissas, 'c', SWAP)  8.78 us
    ppermute x1, starting transfers between devices, body(): lax.ppermute(hidden, 'c', SWAP)  8.6 us
    ppermute x1, waiting for transfers between devices, body(): lax.ppermute(send, ('k', 'p', 'c'), pairs).astype(F32)  8.31 us
  transfers between devices with their start and end apart: 9, of which 6 were waited for; matrix products, arithmetic and copies ran while one was open for 2% of the time, Pallas kernels for 2%

profile of v3, /device:TPU:1, one launch (start us, length us, event | category | flops | bytes accessed | tf_op | source)
XLA Modules:
  0.0 159.7 jit_solution(16172892134353736650)
XLA Ops:
  0.6 0.8 select_reduce_fusion
  1.4 0.1 convert_element_type.46
  1.5 0.1 maximum_bitcast_fusion
  1.6 0.1 broadcast_in_dim.31
  1.6 0.7 pad_maximum_fusion
  2.4 0.8 broadcast_in_dim.32
  3.1 8.8 %collective-permute-start.1 = (bf16[3,896,512]{2,1,0:T(8,128)(2,1)}, bf16[3,896,512]{2,1,0:T(8,128)(2,1)}, u32[]{:S(2)}, u32[]{:S(2)}) collective-permute-start(bf16[3,896,512]{2,1,0:T(8,128)(2,1)} %mant), channel_id=1, source_target_pairs={{0,1},{1,0},{2,3},{3,2},{4,5},{5,4},{6,7},{7,6},{8,9},{9,8},{10,11... | collective-permute-start | bytes 8257544 | tf_op jit(solution)/shard_map/ppermute | solution.py:155
  11.9 5.1 %all-to-all-start = ((bf16[16,16,640]{2,1,0:T(8,128)(2,1)}), bf16[16,16,640]{2,1,0:T(8,128)(2,1)S(1)}, u32[]{:S(2)}, u32[]{:S(2)}) async-start(bf16[16,16,640]{2,1,0:T(8,128)(2,1)} %bitcast.4), calls=%async_computation | async-start | bytes 655360 | tf_op jit(solution)/shard_map/all_to_all | solution.py:153
  17.0 0.8 copy.11
  17.8 2.0 %collective-permute-start = (s32[3,7,4]{2,1,0:T(8,128)S(1)}, s32[3,7,4]{2,1,0:T(8,128)S(1)}, u32[]{:S(2)}, u32[]{:S(2)}) collective-permute-start(s32[3,7,4]{2,1,0:T(8,128)S(1)} %copy.11), channel_id=1, source_target_pairs={{0,1},{1,0},{2,3},{3,2},{4,5},{5,4},{6,7},{7,6},{8,9},{9,8},{10,11... | collective-permute-start | bytes 1016 | tf_op jit(solution)/shard_map/ppermute | solution.py:155
  19.8 0.1 pad_add_fusion.place
  19.9 1.8 %copy-done.2 = bf16[3,896,512]{2,1,0:T(8,128)(2,1)S(1)} copy-done((bf16[3,896,512]{2,1,0:T(8,128)(2,1)S(1)}, bf16[3,896,512]{2,1,0:T(8,128)(2,1)}, u32[]{:S(2)}) %copy-start.2) | copy-done | bytes 2752536
  21.7 1.3 dequant_own.1.own
  23.0 0.0 collective-permute-done
  23.0 0.0 collective-permute-done.1.mant
  23.0 2.3 %dequant_other.1.other = bf16[3,896,512]{2,1,0:T(8,128)(2,1)S(1)} custom-call(f32[3,7,4]{2,1,0:T(8,128)S(1)} %fusion.7.scale, bf16[3,896,512]{2,1,0:T(8,128)(2,1)} %collective-permute-done.1.mant), custom_call_target="tpu_custom_call" | custom-call | flops 1376256 | bytes 5505024 | tf_op jit(solution)/shard_map/dequant_other/pallas_call | solution.py:21
  25.3 0.0 copy-start
  25.3 1.5 copy-done
  26.9 3.2 %all-to-all-done.near = bf16[16,16,640]{2,1,0:T(8,128)(2,1)S(1)} async-done(((bf16[16,16,640]{2,1,0:T(8,128)(2,1)}), bf16[16,16,640]{2,1,0:T(8,128)(2,1)S(1)}, u32[]{:S(2)}, u32[]{:S(2)}) %all-to-all-start) | async-done | bytes 327712 | tf_op jit(solution)/shard_map/all_to_all | solution.py:153
  30.1 0.7 spread.1
  30.8 19.4 %all_to_all.30 = bf16[4,8,16,1024]{3,2,1,0:T(8,128)(2,1)S(1)} all-to-all(bf16[4,8,16,1024]{3,2,1,0:T(8,128)(2,1)S(1)} %spread.1), channel_id=1, replica_groups=mesh['z'=8,'x'=4,'k'=4,'p'=2,'c'=2] {'x'}, dimensions={0} | all-to-all | bytes 2097152 | tf_op jit(solution)/shard_map/all_to_all | solution.py:169
  50.2 0.0 copy-done.1
  50.2 1.8 %project.1 = (bf16[256,512]{1,0:T(8,128)(2,1)S(1)}, bf16[256,512]{1,0:T(8,128)(2,1)S(1)}, bf16[4,96,896]{2,1,0:T(8,128)(2,1)S(1)}, bf16[4,96,896]{2,1,0:T(8,128)(2,1)S(1)}) custom-call(s32[1]{0:T(128)} %bitcast.5.part, bf16[32,16,1024]{2,1,0:T(8,128)(2,1)S(1)} %bitcast.15, bf16[3,896,512]{2,1,0:T(8,128)(2,1)S(1)} %dequant_own.1.own, ...), custom_call_target="tpu_custom_call" | custom-call | flops 1409286144 | bytes 10485760 | tf_op jit(solution)/shard_map/project/pallas_call | solution.py:21
  52.1 0.0 copy-start.3
  52.1 5.1 %collective-permute-start.2 = (bf16[4,96,896]{2,1,0:T(8,128)(2,1)S(1)}, bf16[4,96,896]{2,1,0:T(8,128)(2,1)S(1)}, u32[]{:S(2)}, u32[]{:S(2)}) collective-permute-start(bf16[4,96,896]{2,1,0:T(8,128)(2,1)S(1)} %get-tuple-element.29), channel_id=1, source_target_pairs={{0,2},{2,0},{4,6},{6,4},{8,10},{10,8},{12,14},{14,12},{1,15},{3,5}... | collective-permute-start | bytes 2064392 | tf_op jit(solution)/shard_map/ppermute | solution.py:179
  57.2 8.3 %collective-permute-done.2 = bf16[4,96,896]{2,1,0:T(8,128)(2,1)S(1)} collective-permute-done((bf16[4,96,896]{2,1,0:T(8,128)(2,1)S(1)}, bf16[4,96,896]{2,1,0:T(8,128)(2,1)S(1)}, u32[]{:S(2)}, u32[]{:S(2)}) %collective-permute-start.2) | collective-permute-done | bytes 688160 | tf_op jit(solution)/shard_map/ppermute | solution.py:179
  65.5 0.2 add_convert_fusion
  65.7 25.1 %all_to_all.31.parts = bf16[4,96,896]{2,1,0:T(8,128)(2,1)S(1)} all-to-all(bf16[4,96,896]{2,1,0:T(8,128)(2,1)S(1)} %add_convert_fusion), channel_id=1, replica_groups=mesh['z'=8,'x'=4,'k'=4,'p'=2,'c'=2] {'k'}, dimensions={0} | all-to-all | bytes 1376256 | tf_op jit(solution)/shard_map/all_to_all | solution.py:180
  90.8 0.1 activate.1
  90.9 19.0 %all_to_all.32.acts = bf16[4,96,896]{2,1,0:T(8,128)(2,1)S(1)} all-to-all(bf16[4,96,896]{2,1,0:T(8,128)(2,1)S(1)} %activate.1), channel_id=1, replica_groups=mesh['z'=8,'x'=4,'k'=4,'p'=2,'c'=2] {'k'}, dimensions={0} | all-to-all | bytes 1376256 | tf_op jit(solution)/shard_map/all_to_all | solution.py:182
  109.9 0.1 fusion.9
  110.0 1.9 %collective-permute-start.4 = (bf16[2,96,896]{2,1,0:T(8,128)(2,1)S(1)}, bf16[2,96,896]{2,1,0:T(8,128)(2,1)S(1)}, u32[]{:S(2)}, u32[]{:S(2)}) collective-permute-start(bf16[2,96,896]{2,1,0:T(8,128)(2,1)S(1)} %get-tuple-element.37), channel_id=1, source_target_pairs={{0,14},{2,4},{4,2},{6,8},{8,6},{10,12},{12,10},{14,0},{1,15},{3,5}... | collective-permute-start | bytes 1032200 | tf_op jit(solution)/shard_map/ppermute | solution.py:144
  111.9 1.9 %collective-permute-start.3 = (bf16[2,96,896]{2,1,0:T(8,128)(2,1)S(1)}, bf16[2,96,896]{2,1,0:T(8,128)(2,1)S(1)}, u32[]{:S(2)}, u32[]{:S(2)}) collective-permute-start(bf16[2,96,896]{2,1,0:T(8,128)(2,1)S(1)} %get-tuple-element.38), channel_id=1, source_target_pairs={{0,2},{2,0},{4,6},{6,4},{8,10},{10,8},{12,14},{14,12},{1,3},{3,1},... | collective-permute-start | bytes 1032200 | tf_op jit(solution)/shard_map/ppermute | solution.py:144
  113.8 5.3 %collective-permute-done.4.low = bf16[2,96,896]{2,1,0:T(8,128)(2,1)S(1)} collective-permute-done((bf16[2,96,896]{2,1,0:T(8,128)(2,1)S(1)}, bf16[2,96,896]{2,1,0:T(8,128)(2,1)S(1)}, u32[]{:S(2)}, u32[]{:S(2)}) %collective-permute-start.4) | collective-permute-done | bytes 344096 | tf_op jit(solution)/shard_map/ppermute | solution.py:144
  119.2 0.7 collective-permute-done.3.top
  119.9 1.8 %expand.1 = (bf16[32,16,1024]{2,1,0:T(8,128)(2,1)S(1)}, bf16[256,896]{1,0:T(8,128)(2,1)S(1)}) custom-call(s32[1]{0:T(128)} %bitcast.5.part, bf16[4,96,896]{2,1,0:T(8,128)(2,1)S(1)} %all_to_all.32.acts, bf16[2,96,896]{2,1,0:T(8,128)(2,1)S(1)} %collective-permute-done.3.top, bf16[2,96,896]{2,1,0:T(8,128)(2,1)S(1)} %collective-permute-done.4.low, ...), custom_call_target="tpu_custom_call" | custom-call | flops 1409286144 | bytes 10485760 | tf_op jit(solution)/shard_map/expand/pallas_call | solution.py:21
  121.7 0.0 copy-start.4
  121.7 12.3 %all_to_all.33.terms = bf16[4,8,16,1024]{3,2,1,0:T(8,128)(2,1)S(1)} all-to-all(bf16[4,8,16,1024]{3,2,1,0:T(8,128)(2,1)S(1)} %bitcast.16), channel_id=1, replica_groups=mesh['z'=8,'x'=4,'k'=4,'p'=2,'c'=2] {'x'}, dimensions={0} | all-to-all | bytes 2097152 | tf_op jit(solution)/shard_map/all_to_all | solution.py:187
  134.0 0.8 gather_sum.1
  134.9 8.6 %collective-permute-start.5 = (bf16[256,896]{1,0:T(8,128)(2,1)S(1)}, bf16[256,896]{1,0:T(8,128)(2,1)S(1)}, u32[]{:S(2)}, u32[]{:S(2)}) collective-permute-start(bf16[256,896]{1,0:T(8,128)(2,1)S(1)} %get-tuple-element.34), channel_id=1, source_target_pairs={{0,1},{1,0},{2,3},{3,2},{4,5},{5,4},{6,7},{7,6},{8,9},{9,8},{10,11... | collective-permute-start | bytes 1376264 | tf_op jit(solution)/shard_map/ppermute | solution.py:197
  143.5 3.8 %all-to-all-start.5 = ((bf16[16,16,512]{2,1,0:T(8,128)(2,1)}), bf16[16,16,512]{2,1,0:T(8,128)(2,1)S(1)}, u32[]{:S(2)}, u32[]{:S(2)}) async-start(bf16[16,16,512]{2,1,0:T(8,128)(2,1)} %gather_sum.1), calls=%async_computation.5 | async-start | bytes 524288 | tf_op jit(solution)/shard_map/all_to_all | solution.py:191
  147.3 0.0 copy-done.4
  147.3 2.0 %collective-permute-start.6 = (bf16[256,512]{1,0:T(8,128)(2,1)S(1)}, bf16[256,512]{1,0:T(8,128)(2,1)S(1)}, u32[]{:S(2)}, u32[]{:S(2)}) collective-permute-start(bf16[256,512]{1,0:T(8,128)(2,1)S(1)} %copy-done.4), channel_id=1, source_target_pairs={{0,1},{1,0},{2,3},{3,2},{4,5},{5,4},{6,7},{7,6},{8,9},{9,8},{10,11... | collective-permute-start | bytes 786440 | tf_op jit(solution)/shard_map/ppermute | solution.py:197
  149.3 1.4 collective-permute-done.6
  150.7 0.0 collective-permute-done.5
  150.7 1.6 multiply_convert_fusion
  152.3 6.7 %all-to-all-done.5 = bf16[16,16,512]{2,1,0:T(8,128)(2,1)S(1)} async-done(((bf16[16,16,512]{2,1,0:T(8,128)(2,1)}), bf16[16,16,512]{2,1,0:T(8,128)(2,1)S(1)}, u32[]{:S(2)}, u32[]{:S(2)}) %all-to-all-start.5) | async-done | bytes 262176 | tf_op jit(solution)/shard_map/all_to_all | solution.py:191
  159.0 0.6 slice_bitcast_fusion
  (7 shorter events, 0.1 us)
Async XLA Ops:
  3.1 19.9 %collective-permute-start.1 = (bf16[3,896,512]{2,1,0:T(8,128)(2,1)}, bf16[3,896,512]{2,1,0:T(8,128)(2,1)}, u32[]{:S(2)}, u32[]{:S(2)}) collective-permute-start(bf16[3,896,512]{2,1,0:T(8,128)(2,1)} %mant), channel_id=1, source_target_pairs={{0,1},{1,0},{2,3},{3,2},{4,5},{5,4},{6,7},{7,6},{8,9},{9,8},{10,11... | collective-permute-start | bytes 8257544 | tf_op jit(solution)/shard_map/ppermute | solution.py:155
  11.9 18.1 %all-to-all-start = ((bf16[16,16,640]{2,1,0:T(8,128)(2,1)}), bf16[16,16,640]{2,1,0:T(8,128)(2,1)S(1)}, u32[]{:S(2)}, u32[]{:S(2)}) async-start(bf16[16,16,640]{2,1,0:T(8,128)(2,1)} %bitcast.4), calls=%async_computation | async-start | bytes 655360 | tf_op jit(solution)/shard_map/all_to_all | solution.py:153
  17.8 5.2 %collective-permute-start = (s32[3,7,4]{2,1,0:T(8,128)S(1)}, s32[3,7,4]{2,1,0:T(8,128)S(1)}, u32[]{:S(2)}, u32[]{:S(2)}) collective-permute-start(s32[3,7,4]{2,1,0:T(8,128)S(1)} %copy.11), channel_id=1, source_target_pairs={{0,1},{1,0},{2,3},{3,2},{4,5},{5,4},{6,7},{7,6},{8,9},{9,8},{10,11... | collective-permute-start | bytes 1016 | tf_op jit(solution)/shard_map/ppermute | solution.py:155
  19.9 1.8 %copy-start.2 = (bf16[3,896,512]{2,1,0:T(8,128)(2,1)S(1)}, bf16[3,896,512]{2,1,0:T(8,128)(2,1)}, u32[]{:S(2)}) copy-start(bf16[3,896,512]{2,1,0:T(8,128)(2,1)} %mant) | copy-start | bytes 8257540
  25.3 1.5 copy-start
  30.1 20.2 %copy-start.1 = (bf16[3,896,512]{2,1,0:T(8,128)(2,1)S(1)}, bf16[3,896,512]{2,1,0:T(8,128)(2,1)}, u32[]{:S(2)}) copy-start(bf16[3,896,512]{2,1,0:T(8,128)(2,1)} %copy-done) | copy-start | bytes 8257540
  52.1 38.9 %copy-start.3 = (bf16[256,512]{1,0:T(8,128)(2,1)}, bf16[256,512]{1,0:T(8,128)(2,1)S(1)}, u32[]{:S(2)}) copy-start(bf16[256,512]{1,0:T(8,128)(2,1)S(1)} %get-tuple-element.36) | copy-start | bytes 786436
  52.1 13.4 %collective-permute-start.2 = (bf16[4,96,896]{2,1,0:T(8,128)(2,1)S(1)}, bf16[4,96,896]{2,1,0:T(8,128)(2,1)S(1)}, u32[]{:S(2)}, u32[]{:S(2)}) collective-permute-start(bf16[4,96,896]{2,1,0:T(8,128)(2,1)S(1)} %get-tuple-element.29), channel_id=1, source_target_pairs={{0,2},{2,0},{4,6},{6,4},{8,10},{10,8},{12,14},{14,12},{1,15},{3,5}... | collective-permute-start | bytes 2064392 | tf_op jit(solution)/shard_map/ppermute | solution.py:179
  110.0 9.2 %collective-permute-start.4 = (bf16[2,96,896]{2,1,0:T(8,128)(2,1)S(1)}, bf16[2,96,896]{2,1,0:T(8,128)(2,1)S(1)}, u32[]{:S(2)}, u32[]{:S(2)}) collective-permute-start(bf16[2,96,896]{2,1,0:T(8,128)(2,1)S(1)} %get-tuple-element.37), channel_id=1, source_target_pairs={{0,14},{2,4},{4,2},{6,8},{8,6},{10,12},{12,10},{14,0},{1,15},{3,5}... | collective-permute-start | bytes 1032200 | tf_op jit(solution)/shard_map/ppermute | solution.py:144
  111.9 8.0 %collective-permute-start.3 = (bf16[2,96,896]{2,1,0:T(8,128)(2,1)S(1)}, bf16[2,96,896]{2,1,0:T(8,128)(2,1)S(1)}, u32[]{:S(2)}, u32[]{:S(2)}) collective-permute-start(bf16[2,96,896]{2,1,0:T(8,128)(2,1)S(1)} %get-tuple-element.38), channel_id=1, source_target_pairs={{0,2},{2,0},{4,6},{6,4},{8,10},{10,8},{12,14},{14,12},{1,3},{3,1},... | collective-permute-start | bytes 1032200 | tf_op jit(solution)/shard_map/ppermute | solution.py:144
  121.7 25.6 %copy-start.4 = (bf16[256,512]{1,0:T(8,128)(2,1)S(1)}, bf16[256,512]{1,0:T(8,128)(2,1)}, u32[]{:S(2)}) copy-start(bf16[256,512]{1,0:T(8,128)(2,1)} %copy-done.3) | copy-start | bytes 786436
  134.9 15.9 %collective-permute-start.5 = (bf16[256,896]{1,0:T(8,128)(2,1)S(1)}, bf16[256,896]{1,0:T(8,128)(2,1)S(1)}, u32[]{:S(2)}, u32[]{:S(2)}) collective-permute-start(bf16[256,896]{1,0:T(8,128)(2,1)S(1)} %get-tuple-element.34), channel_id=1, source_target_pairs={{0,1},{1,0},{2,3},{3,2},{4,5},{5,4},{6,7},{7,6},{8,9},{9,8},{10,11... | collective-permute-start | bytes 1376264 | tf_op jit(solution)/shard_map/ppermute | solution.py:197
  143.5 15.5 %all-to-all-start.5 = ((bf16[16,16,512]{2,1,0:T(8,128)(2,1)}), bf16[16,16,512]{2,1,0:T(8,128)(2,1)S(1)}, u32[]{:S(2)}, u32[]{:S(2)}) async-start(bf16[16,16,512]{2,1,0:T(8,128)(2,1)} %gather_sum.1), calls=%async_computation.5 | async-start | bytes 524288 | tf_op jit(solution)/shard_map/all_to_all | solution.py:191
  147.3 3.4 %collective-permute-start.6 = (bf16[256,512]{1,0:T(8,128)(2,1)S(1)}, bf16[256,512]{1,0:T(8,128)(2,1)S(1)}, u32[]{:S(2)}, u32[]{:S(2)}) collective-permute-start(bf16[256,512]{1,0:T(8,128)(2,1)S(1)} %copy-done.4), channel_id=1, source_target_pairs={{0,1},{1,0},{2,3},{3,2},{4,5},{5,4},{6,7},{7,6},{8,9},{9,8},{10,11... | collective-permute-start | bytes 786440 | tf_op jit(solution)/shard_map/ppermute | solution.py:197

commit v4 on v3

--- a/solution.py
+++ b/solution.py
@@ -38,13 +38,16 @@
                 out[at] = (mant[at].astype(F32) * scale[m, r, c]).astype(BF16)
 
 
-def spread_kernel(place, near, out):
+def spread_kernel(place, class_bands, near, out):
     copies, chips, _, width = out.shape
     half = width // 2
     for i in range(chips):
         own = near[2 * i + place[0], :, :half].astype(F32)
         other = near[2 * i + 1 - place[0], :, :half].astype(F32)
-        limit = near[2 * i, :, half:].astype(F32)[:, :1]
+        kind = near[2 * i, :, half:].astype(F32)[:, :1]
+        limit = jnp.zeros_like(kind)
+        for j in range(class_bands.shape[0]):
+            limit = jnp.where(kind == j, class_bands[j].astype(F32), limit)
         for x in range(copies):
             keep = (place[1] * copies + x).astype(F32) < limit
             out[x, i, :, :half] = jnp.where(keep, own, 0.0).astype(BF16)
@@ -143,9 +146,8 @@
     def swap_near(top, low):
         return (lax.ppermute(top, ("k", "p"), left_pairs), lax.ppermute(low, ("k", "p"), right_pairs))
 
-    lookup = token_class[:, None] == jnp.arange(class_bands.shape[0], dtype=jnp.int32)[None, :]
-    used = jnp.sum(jnp.where(lookup, class_bands[None, :], 0), axis=1).astype(BF16).reshape(2, mine, 1)
-    tail = jnp.broadcast_to(jnp.concatenate([used, used], axis=1), (2, rows, BLOCK))
+    kind = token_class.astype(BF16).reshape(2, mine, 1)
+    tail = jnp.broadcast_to(jnp.concatenate([kind, kind], axis=1), (2, rows, BLOCK))
     pair = jnp.concatenate([tokens.reshape(2, mine, half), cotangent.reshape(2, mine, half)], axis=1)
     pair = jnp.concatenate([pair, tail], axis=2)
     pair = jnp.broadcast_to(pair[None], (zs, 2, rows, half + BLOCK)).reshape(zs * 2, rows, half + BLOCK)
@@ -164,8 +166,8 @@
 
     place = jnp.stack([core, lax.axis_index("z")])
     near, own, other, odd, place = lax.optimization_barrier((near, own, other, odd, place))
-    masked = call(spread_kernel, "spread", jax.ShapeDtypeStruct((xs, zs, rows, 2 * half), BF16), (place, near),
-                  smem=(0,), moved=2 << 20)
+    masked = call(spread_kernel, "spread", jax.ShapeDtypeStruct((xs, zs, rows, 2 * half), BF16), (place, class_bands, near),
+                  smem=(0, 1), moved=2 << 20)
     gathered = lax.all_to_all(masked, "x", 0, 0, tiled=True).reshape(bands, rows, 2 * half)
 
     work = count * mats * units * 2 * half

time: 161 us -> 160 us (level)
    unnamed x10 -> x12, local copies, waits for them, and re-layouts: 3.33 us -> 3.33 us
where the time goes in v4:
time: 160 us
  blocking collectives  75.8 us (47%)
  starting transfers between devices  39.2 us (25%)
  waiting for transfers between devices  25.6 us (16%)
  Pallas kernels  8.98 us (6%)
  local copies, waits for them, and re-layouts  5.7 us (4%)
  other arithmetic  1.78 us (1%)
  matrix products  1.6 us (1%)
    all_to_all x1, blocking collectives, body(): parts = lax.all_to_all(parts, 'k', 0, 0, tiled=True)  25.1 us
    all_to_all x1, blocking collectives, body(): lax.all_to_all(masked, 'x', 0, 0, tiled=True).reshape(bands, rows, 2 * half)  19.4 us
    all_to_all x1, blocking collectives, body(): acts = lax.all_to_all(acts, 'k', 0, 0, tiled=True)  18.9 us
    all_to_all x1, blocking collectives, body(): lax.all_to_all(terms.reshape(xs, zs, rows, 2 * half), 'x', 0, 0, tiled=True)  12.3 us
    pallas_call x7, Pallas kernels, call(): pl.pallas_call(kernel, name=name, out_shape=outs, in_specs=[scalar if i i...  8.98 us
    ppermute x1, starting transfers between devices, body(): lax.ppermute(mantissas, 'c', SWAP)  8.78 us
    ppermute x1, starting transfers between devices, body(): lax.ppermute(hidden, 'c', SWAP)  8.61 us
    ppermute x1, waiting for transfers between devices, body(): lax.ppermute(send, ('k', 'p', 'c'), pairs).astype(F32)  8.31 us
  transfers between devices with their start and end apart: 9, of which 6 were waited for; matrix products, arithmetic and copies ran while one was open for 2% of the time, Pallas kernels for 2%

profile of v4, /device:TPU:1, one launch (start us, length us, event | category | flops | bytes accessed | tf_op | source)
XLA Modules:
  0.0 159.5 jit_solution(2812525783728714199)
XLA Ops:
  0.6 0.7 convert_element_type.35
  1.3 0.1 reshape.43
  1.4 0.1 maximum_bitcast_fusion
  1.5 0.1 broadcast_in_dim.14
  1.5 0.7 pad_maximum_fusion
  2.3 0.8 broadcast_in_dim.15
  3.0 8.8 %collective-permute-start.1 = (bf16[3,896,512]{2,1,0:T(8,128)(2,1)}, bf16[3,896,512]{2,1,0:T(8,128)(2,1)}, u32[]{:S(2)}, u32[]{:S(2)}) collective-permute-start(bf16[3,896,512]{2,1,0:T(8,128)(2,1)} %mant), channel_id=1, source_target_pairs={{0,1},{1,0},{2,3},{3,2},{4,5},{5,4},{6,7},{7,6},{8,9},{9,8},{10,11... | collective-permute-start | bytes 8257544 | tf_op jit(solution)/shard_map/ppermute | solution.py:157
  11.8 5.1 %all-to-all-start = ((bf16[16,16,640]{2,1,0:T(8,128)(2,1)}), bf16[16,16,640]{2,1,0:T(8,128)(2,1)S(1)}, u32[]{:S(2)}, u32[]{:S(2)}) async-start(bf16[16,16,640]{2,1,0:T(8,128)(2,1)} %bitcast.4), calls=%async_computation | async-start | bytes 655360 | tf_op jit(solution)/shard_map/all_to_all | solution.py:155
  16.9 0.8 copy.9
  17.7 2.0 %collective-permute-start = (s32[3,7,4]{2,1,0:T(8,128)S(1)}, s32[3,7,4]{2,1,0:T(8,128)S(1)}, u32[]{:S(2)}, u32[]{:S(2)}) collective-permute-start(s32[3,7,4]{2,1,0:T(8,128)S(1)} %copy.9), channel_id=1, source_target_pairs={{0,1},{1,0},{2,3},{3,2},{4,5},{5,4},{6,7},{7,6},{8,9},{9,8},{10,11... | collective-permute-start | bytes 1016 | tf_op jit(solution)/shard_map/ppermute | solution.py:157
  19.7 0.1 pad_add_fusion.place
  19.8 1.8 %copy-done.2 = bf16[3,896,512]{2,1,0:T(8,128)(2,1)S(1)} copy-done((bf16[3,896,512]{2,1,0:T(8,128)(2,1)S(1)}, bf16[3,896,512]{2,1,0:T(8,128)(2,1)}, u32[]{:S(2)}) %copy-start.2) | copy-done | bytes 2752536
  21.6 1.3 dequant_own.1.own
  22.9 0.0 collective-permute-done
  22.9 0.0 copy-start.3
  22.9 0.0 collective-permute-done.1.mant
  22.9 2.3 %dequant_other.1.other = bf16[3,896,512]{2,1,0:T(8,128)(2,1)S(1)} custom-call(f32[3,7,4]{2,1,0:T(8,128)S(1)} %fusion.7.scale, bf16[3,896,512]{2,1,0:T(8,128)(2,1)} %collective-permute-done.1.mant), custom_call_target="tpu_custom_call" | custom-call | flops 1376256 | bytes 5505024 | tf_op jit(solution)/shard_map/dequant_other/pallas_call | solution.py:21
  25.2 0.0 copy-start
  25.2 1.5 copy-done
  26.8 3.2 %all-to-all-done.near = bf16[16,16,640]{2,1,0:T(8,128)(2,1)S(1)} async-done(((bf16[16,16,640]{2,1,0:T(8,128)(2,1)}), bf16[16,16,640]{2,1,0:T(8,128)(2,1)S(1)}, u32[]{:S(2)}, u32[]{:S(2)}) %all-to-all-start) | async-done | bytes 327712 | tf_op jit(solution)/shard_map/all_to_all | solution.py:155
  30.0 0.7 spread.1
  30.7 19.4 %all_to_all.30 = bf16[4,8,16,1024]{3,2,1,0:T(8,128)(2,1)S(1)} all-to-all(bf16[4,8,16,1024]{3,2,1,0:T(8,128)(2,1)S(1)} %spread.1), channel_id=1, replica_groups=mesh['z'=8,'x'=4,'k'=4,'p'=2,'c'=2] {'x'}, dimensions={0} | all-to-all | bytes 2097152 | tf_op jit(solution)/shard_map/all_to_all | solution.py:171
  50.1 0.0 copy-done.1
  50.1 1.8 %project.1 = (bf16[256,512]{1,0:T(8,128)(2,1)S(1)}, bf16[256,512]{1,0:T(8,128)(2,1)S(1)}, bf16[4,96,896]{2,1,0:T(8,128)(2,1)S(1)}, bf16[4,96,896]{2,1,0:T(8,128)(2,1)S(1)}) custom-call(s32[1]{0:T(128)} %bitcast.5.part, bf16[32,16,1024]{2,1,0:T(8,128)(2,1)S(1)} %bitcast.15, bf16[3,896,512]{2,1,0:T(8,128)(2,1)S(1)} %dequant_own.1.own, ...), custom_call_target="tpu_custom_call" | custom-call | flops 1409286144 | bytes 10485760 | tf_op jit(solution)/shard_map/project/pallas_call | solution.py:21
  52.0 0.0 copy-start.4
  52.0 5.1 %collective-permute-start.2 = (bf16[4,96,896]{2,1,0:T(8,128)(2,1)S(1)}, bf16[4,96,896]{2,1,0:T(8,128)(2,1)S(1)}, u32[]{:S(2)}, u32[]{:S(2)}) collective-permute-start(bf16[4,96,896]{2,1,0:T(8,128)(2,1)S(1)} %get-tuple-element.29), channel_id=1, source_target_pairs={{0,2},{2,0},{4,6},{6,4},{8,10},{10,8},{12,14},{14,12},{1,15},{3,5}... | collective-permute-start | bytes 2064392 | tf_op jit(solution)/shard_map/ppermute | solution.py:181
  57.1 8.3 %collective-permute-done.2 = bf16[4,96,896]{2,1,0:T(8,128)(2,1)S(1)} collective-permute-done((bf16[4,96,896]{2,1,0:T(8,128)(2,1)S(1)}, bf16[4,96,896]{2,1,0:T(8,128)(2,1)S(1)}, u32[]{:S(2)}, u32[]{:S(2)}) %collective-permute-start.2) | collective-permute-done | bytes 688160 | tf_op jit(solution)/shard_map/ppermute | solution.py:181
  65.4 0.2 add_convert_fusion
  65.6 25.1 %all_to_all.31.parts = bf16[4,96,896]{2,1,0:T(8,128)(2,1)S(1)} all-to-all(bf16[4,96,896]{2,1,0:T(8,128)(2,1)S(1)} %add_convert_fusion), channel_id=1, replica_groups=mesh['z'=8,'x'=4,'k'=4,'p'=2,'c'=2] {'k'}, dimensions={0} | all-to-all | bytes 1376256 | tf_op jit(solution)/shard_map/all_to_all | solution.py:182
  90.7 0.1 activate.1
  90.8 18.9 %all_to_all.32.acts = bf16[4,96,896]{2,1,0:T(8,128)(2,1)S(1)} all-to-all(bf16[4,96,896]{2,1,0:T(8,128)(2,1)S(1)} %activate.1), channel_id=1, replica_groups=mesh['z'=8,'x'=4,'k'=4,'p'=2,'c'=2] {'k'}, dimensions={0} | all-to-all | bytes 1376256 | tf_op jit(solution)/shard_map/all_to_all | solution.py:184
  109.8 0.1 fusion.9
  109.8 1.9 %collective-permute-start.4 = (bf16[2,96,896]{2,1,0:T(8,128)(2,1)S(1)}, bf16[2,96,896]{2,1,0:T(8,128)(2,1)S(1)}, u32[]{:S(2)}, u32[]{:S(2)}) collective-permute-start(bf16[2,96,896]{2,1,0:T(8,128)(2,1)S(1)} %get-tuple-element.37), channel_id=1, source_target_pairs={{0,14},{2,4},{4,2},{6,8},{8,6},{10,12},{12,10},{14,0},{1,15},{3,5}... | collective-permute-start | bytes 1032200 | tf_op jit(solution)/shard_map/ppermute | solution.py:147
  111.8 1.9 %collective-permute-start.3 = (bf16[2,96,896]{2,1,0:T(8,128)(2,1)S(1)}, bf16[2,96,896]{2,1,0:T(8,128)(2,1)S(1)}, u32[]{:S(2)}, u32[]{:S(2)}) collective-permute-start(bf16[2,96,896]{2,1,0:T(8,128)(2,1)S(1)} %get-tuple-element.38), channel_id=1, source_target_pairs={{0,2},{2,0},{4,6},{6,4},{8,10},{10,8},{12,14},{14,12},{1,3},{3,1},... | collective-permute-start | bytes 1032200 | tf_op jit(solution)/shard_map/ppermute | solution.py:147
  113.7 5.3 %collective-permute-done.4.low = bf16[2,96,896]{2,1,0:T(8,128)(2,1)S(1)} collective-permute-done((bf16[2,96,896]{2,1,0:T(8,128)(2,1)S(1)}, bf16[2,96,896]{2,1,0:T(8,128)(2,1)S(1)}, u32[]{:S(2)}, u32[]{:S(2)}) %collective-permute-start.4) | collective-permute-done | bytes 344096 | tf_op jit(solution)/shard_map/ppermute | solution.py:147
  119.1 0.7 collective-permute-done.3.top
  119.8 1.8 %expand.1 = (bf16[32,16,1024]{2,1,0:T(8,128)(2,1)S(1)}, bf16[256,896]{1,0:T(8,128)(2,1)S(1)}) custom-call(s32[1]{0:T(128)} %bitcast.5.part, bf16[4,96,896]{2,1,0:T(8,128)(2,1)S(1)} %all_to_all.32.acts, bf16[2,96,896]{2,1,0:T(8,128)(2,1)S(1)} %collective-permute-done.3.top, bf16[2,96,896]{2,1,0:T(8,128)(2,1)S(1)} %collective-permute-done.4.low, ...), custom_call_target="tpu_custom_call" | custom-call | flops 1409286144 | bytes 10485760 | tf_op jit(solution)/shard_map/expand/pallas_call | solution.py:21
  121.6 0.0 copy-start.5
  121.6 12.3 %all_to_all.33.terms = bf16[4,8,16,1024]{3,2,1,0:T(8,128)(2,1)S(1)} all-to-all(bf16[4,8,16,1024]{3,2,1,0:T(8,128)(2,1)S(1)} %bitcast.16), channel_id=1, replica_groups=mesh['z'=8,'x'=4,'k'=4,'p'=2,'c'=2] {'x'}, dimensions={0} | all-to-all | bytes 2097152 | tf_op jit(solution)/shard_map/all_to_all | solution.py:189
  133.9 0.8 gather_sum.1
  134.7 8.6 %collective-permute-start.5 = (bf16[256,896]{1,0:T(8,128)(2,1)S(1)}, bf16[256,896]{1,0:T(8,128)(2,1)S(1)}, u32[]{:S(2)}, u32[]{:S(2)}) collective-permute-start(bf16[256,896]{1,0:T(8,128)(2,1)S(1)} %get-tuple-element.34), channel_id=1, source_target_pairs={{0,1},{1,0},{2,3},{3,2},{4,5},{5,4},{6,7},{7,6},{8,9},{9,8},{10,11... | collective-permute-start | bytes 1376264 | tf_op jit(solution)/shard_map/ppermute | solution.py:199
  143.4 3.8 %all-to-all-start.5 = ((bf16[16,16,512]{2,1,0:T(8,128)(2,1)}), bf16[16,16,512]{2,1,0:T(8,128)(2,1)S(1)}, u32[]{:S(2)}, u32[]{:S(2)}) async-start(bf16[16,16,512]{2,1,0:T(8,128)(2,1)} %gather_sum.1), calls=%async_computation.5 | async-start | bytes 524288 | tf_op jit(solution)/shard_map/all_to_all | solution.py:193
  147.2 2.0 %collective-permute-start.6 = (bf16[256,512]{1,0:T(8,128)(2,1)S(1)}, bf16[256,512]{1,0:T(8,128)(2,1)S(1)}, u32[]{:S(2)}, u32[]{:S(2)}) collective-permute-start(bf16[256,512]{1,0:T(8,128)(2,1)S(1)} %copy-done.5), channel_id=1, source_target_pairs={{0,1},{1,0},{2,3},{3,2},{4,5},{5,4},{6,7},{7,6},{8,9},{9,8},{10,11... | collective-permute-start | bytes 786440 | tf_op jit(solution)/shard_map/ppermute | solution.py:199
  149.2 1.4 collective-permute-done.6
  150.6 0.0 collective-permute-done.5
  150.6 1.6 multiply_convert_fusion
  152.2 6.7 %all-to-all-done.5 = bf16[16,16,512]{2,1,0:T(8,128)(2,1)S(1)} async-done(((bf16[16,16,512]{2,1,0:T(8,128)(2,1)}), bf16[16,16,512]{2,1,0:T(8,128)(2,1)S(1)}, u32[]{:S(2)}, u32[]{:S(2)}) %all-to-all-start.5) | async-done | bytes 262176 | tf_op jit(solution)/shard_map/all_to_all | solution.py:193
  158.9 0.6 slice_bitcast_fusion
  (8 shorter events, 0.1 us)
Async XLA Ops:
  3.0 19.9 %collective-permute-start.1 = (bf16[3,896,512]{2,1,0:T(8,128)(2,1)}, bf16[3,896,512]{2,1,0:T(8,128)(2,1)}, u32[]{:S(2)}, u32[]{:S(2)}) collective-permute-start(bf16[3,896,512]{2,1,0:T(8,128)(2,1)} %mant), channel_id=1, source_target_pairs={{0,1},{1,0},{2,3},{3,2},{4,5},{5,4},{6,7},{7,6},{8,9},{9,8},{10,11... | collective-permute-start | bytes 8257544 | tf_op jit(solution)/shard_map/ppermute | solution.py:157
  11.8 18.1 %all-to-all-start = ((bf16[16,16,640]{2,1,0:T(8,128)(2,1)}), bf16[16,16,640]{2,1,0:T(8,128)(2,1)S(1)}, u32[]{:S(2)}, u32[]{:S(2)}) async-start(bf16[16,16,640]{2,1,0:T(8,128)(2,1)} %bitcast.4), calls=%async_computation | async-start | bytes 655360 | tf_op jit(solution)/shard_map/all_to_all | solution.py:155
  17.7 5.2 %collective-permute-start = (s32[3,7,4]{2,1,0:T(8,128)S(1)}, s32[3,7,4]{2,1,0:T(8,128)S(1)}, u32[]{:S(2)}, u32[]{:S(2)}) collective-permute-start(s32[3,7,4]{2,1,0:T(8,128)S(1)} %copy.9), channel_id=1, source_target_pairs={{0,1},{1,0},{2,3},{3,2},{4,5},{5,4},{6,7},{7,6},{8,9},{9,8},{10,11... | collective-permute-start | bytes 1016 | tf_op jit(solution)/shard_map/ppermute | solution.py:157
  19.8 1.8 %copy-start.2 = (bf16[3,896,512]{2,1,0:T(8,128)(2,1)S(1)}, bf16[3,896,512]{2,1,0:T(8,128)(2,1)}, u32[]{:S(2)}) copy-start(bf16[3,896,512]{2,1,0:T(8,128)(2,1)} %mant) | copy-start | bytes 8257540
  22.9 7.1 %copy-start.3 = (s32[4]{0:T(128)S(1)}, s32[4]{0:T(128)}, u32[]{:S(2)}) copy-start(s32[4]{0:T(128)} %class_bands.1) | copy-start | bytes 52
  25.2 1.5 copy-start
  30.0 20.2 %copy-start.1 = (bf16[3,896,512]{2,1,0:T(8,128)(2,1)S(1)}, bf16[3,896,512]{2,1,0:T(8,128)(2,1)}, u32[]{:S(2)}) copy-start(bf16[3,896,512]{2,1,0:T(8,128)(2,1)} %copy-done) | copy-start | bytes 8257540
  52.0 38.9 %copy-start.4 = (bf16[256,512]{1,0:T(8,128)(2,1)}, bf16[256,512]{1,0:T(8,128)(2,1)S(1)}, u32[]{:S(2)}) copy-start(bf16[256,512]{1,0:T(8,128)(2,1)S(1)} %get-tuple-element.36) | copy-start | bytes 786436
  52.0 13.4 %collective-permute-start.2 = (bf16[4,96,896]{2,1,0:T(8,128)(2,1)S(1)}, bf16[4,96,896]{2,1,0:T(8,128)(2,1)S(1)}, u32[]{:S(2)}, u32[]{:S(2)}) collective-permute-start(bf16[4,96,896]{2,1,0:T(8,128)(2,1)S(1)} %get-tuple-element.29), channel_id=1, source_target_pairs={{0,2},{2,0},{4,6},{6,4},{8,10},{10,8},{12,14},{14,12},{1,15},{3,5}... | collective-permute-start | bytes 2064392 | tf_op jit(solution)/shard_map/ppermute | solution.py:181
  109.8 9.2 %collective-permute-start.4 = (bf16[2,96,896]{2,1,0:T(8,128)(2,1)S(1)}, bf16[2,96,896]{2,1,0:T(8,128)(2,1)S(1)}, u32[]{:S(2)}, u32[]{:S(2)}) collective-permute-start(bf16[2,96,896]{2,1,0:T(8,128)(2,1)S(1)} %get-tuple-element.37), channel_id=1, source_target_pairs={{0,14},{2,4},{4,2},{6,8},{8,6},{10,12},{12,10},{14,0},{1,15},{3,5}... | collective-permute-start | bytes 1032200 | tf_op jit(solution)/shard_map/ppermute | solution.py:147
  111.8 8.0 %collective-permute-start.3 = (bf16[2,96,896]{2,1,0:T(8,128)(2,1)S(1)}, bf16[2,96,896]{2,1,0:T(8,128)(2,1)S(1)}, u32[]{:S(2)}, u32[]{:S(2)}) collective-permute-start(bf16[2,96,896]{2,1,0:T(8,128)(2,1)S(1)} %get-tuple-element.38), channel_id=1, source_target_pairs={{0,2},{2,0},{4,6},{6,4},{8,10},{10,8},{12,14},{14,12},{1,3},{3,1},... | collective-permute-start | bytes 1032200 | tf_op jit(solution)/shard_map/ppermute | solution.py:147
  121.6 25.6 %copy-start.5 = (bf16[256,512]{1,0:T(8,128)(2,1)S(1)}, bf16[256,512]{1,0:T(8,128)(2,1)}, u32[]{:S(2)}) copy-start(bf16[256,512]{1,0:T(8,128)(2,1)} %copy-done.4) | copy-start | bytes 786436
  134.7 15.9 %collective-permute-start.5 = (bf16[256,896]{1,0:T(8,128)(2,1)S(1)}, bf16[256,896]{1,0:T(8,128)(2,1)S(1)}, u32[]{:S(2)}, u32[]{:S(2)}) collective-permute-start(bf16[256,896]{1,0:T(8,128)(2,1)S(1)} %get-tuple-element.34), channel_id=1, source_target_pairs={{0,1},{1,0},{2,3},{3,2},{4,5},{5,4},{6,7},{7,6},{8,9},{9,8},{10,11... | collective-permute-start | bytes 1376264 | tf_op jit(solution)/shard_map/ppermute | solution.py:199
  143.4 15.5 %all-to-all-start.5 = ((bf16[16,16,512]{2,1,0:T(8,128)(2,1)}), bf16[16,16,512]{2,1,0:T(8,128)(2,1)S(1)}, u32[]{:S(2)}, u32[]{:S(2)}) async-start(bf16[16,16,512]{2,1,0:T(8,128)(2,1)} %gather_sum.1), calls=%async_computation.5 | async-start | bytes 524288 | tf_op jit(solution)/shard_map/all_to_all | solution.py:193
  147.2 3.4 %collective-permute-start.6 = (bf16[256,512]{1,0:T(8,128)(2,1)S(1)}, bf16[256,512]{1,0:T(8,128)(2,1)S(1)}, u32[]{:S(2)}, u32[]{:S(2)}) collective-permute-start(bf16[256,512]{1,0:T(8,128)(2,1)S(1)} %copy-done.5), channel_id=1, source_target_pairs={{0,1},{1,0},{2,3},{3,2},{4,5},{5,4},{6,7},{7,6},{8,9},{9,8},{10,11... | collective-permute-start | bytes 786440 | tf_op jit(solution)/shard_map/ppermute | solution.py:199
